TPU v7x, 32 devices: a whole 2x2x4 slice. The times are simulated.
32 devices in a mesh: dp: 2 (over x), row: 4 (over z), col: 4 (over y, core).
Axes of the slice: x: 2, y: 2, z: 4, core: 2. Of those that a mesh axis runs over, the one named last changes fastest.
Arguments:
- tokens: bfloat16 [4, 8, 1024, 768], P(None, None, 'col', ('dp', 'row')), may hold values from -6 to 6
- cotangent: bfloat16 [4, 8, 1024, 768], P(None, ('dp', 'row'), 'col'), may hold values from -6 to 6
- lengths: int32 [4, 8], replicated, may hold values from 1 to 1024, 5120 in all within a row
- seq_order: int32 [4, 8], replicated, may hold values from 0 to 7, each once within a row
- w_qkv: bfloat16 [768, 2304], P(('dp', 'row'), 'col'), may hold values from -0.21875 to 0.21875
- w_out: bfloat16 [768, 768], P(('dp', 'row'), 'col'), may hold values from -2 to 2
- w_up: bfloat16 [768, 3072], P(('dp', 'row'), 'col'), may hold values from -0.21875 to 0.21875
- w_down: bfloat16 [3072, 768], P(('dp', 'row'), 'col'), may hold values from -0.109375 to 0.109375
- gain_one: bfloat16 [768], P(('dp', 'row', 'col')), may hold values from 0.5 to 1.5
- shift_one: bfloat16 [768], P(('dp', 'row', 'col')), may hold values from -1 to 1
- gain_two: bfloat16 [768], P(('dp', 'row', 'col')), may hold values from 0.5 to 1.5
- shift_two: bfloat16 [768], P(('dp', 'row', 'col')), may hold values from -1 to 1
Outputs:
- output: bfloat16 [4, 8, 1024, 768], P(None, ('dp', 'row'), 'col')
- tokens_grad: bfloat16 [4, 8, 1024, 768], P(None, None, 'col', ('dp', 'row'))
- w_qkv_grad: float32 [768, 2304], P(('dp', 'row'), 'col')
- w_out_grad: float32 [768, 768], P(('dp', 'row'), 'col')
- w_up_grad: float32 [768, 3072], P(('dp', 'row'), 'col')
- w_down_grad: float32 [3072, 768], P(('dp', 'row'), 'col')
- gain_one_grad: float32 [768], P(('dp', 'row', 'col'))
- shift_one_grad: float32 [768], P(('dp', 'row', 'col'))
- gain_two_grad: float32 [768], P(('dp', 'row', 'col'))
- shift_two_grad: float32 [768], P(('dp', 'row', 'col'))
Inputs may be any that keep to these rules, and one draw needn't show every extreme that they name: `seq_order`: each row is a permutation of the micro-batch's 8 sequences. In every micro-batch the lengths add up to 5120, and the longest is 1024.
All inputs are finite; a program needn't handle non-finite values.
Results may differ from a plain program's by a relative error of at most 0.017.
Values may be sent and summed in bfloat16 or wider, within the bound.
A program may use at most 256 MiB of HBM per device.

v0:
```python
import functools

import jax
import jax.numpy as jnp
from jax import lax
from jax.experimental import pallas as pl
from jax.experimental.pallas import tpu as pltpu
from jax.sharding import PartitionSpec as P

HEAD = 64
NEGATIVE = -1000000000.0
EPSILON = 1e-12
ROOT_HALF = 0.7071067811865476
ROOT_TWO_PI = 0.3989422804014327
MESH = pl.DeviceIdType.MESH
BF = jnp.bfloat16
F32 = jnp.float32
ANY = pl.BlockSpec(memory_space=pl.ANY)
VM = pl.BlockSpec(memory_space=pltpu.VMEM)
SM = pl.BlockSpec(memory_space=pltpu.SMEM)
DMA = pltpu.SemaphoreType.DMA


def aligned(value, step):
    return pl.multiple_of(value, step)


def product(left, right):
    return jnp.dot(left, right, preferred_element_type=F32)


def product_tn(left, right):
    return lax.dot_general(left, right, (((0,), (0,)), ((), ())), preferred_element_type=F32)


def product_nt(left, right):
    return lax.dot_general(left, right, (((1,), (1,)), ((), ())), preferred_element_type=F32)


class Place:
    def __init__(self, n_dp, n_row, n_col):
        self.n_dp, self.n_row, self.n_col = n_dp, n_row, n_col
        self.n = n_dp * n_row * n_col
        self.x = lax.axis_index("dp")
        self.z = lax.axis_index("row")
        self.c = lax.axis_index("col")
        self.y, self.k = self.c // 2, self.c % 2
        self.g = self.x * n_row + self.z
        self.flat = self.g * n_col + self.c

    def of_flat(self, flat):
        group = flat // self.n_col
        return (group // self.n_row, group % self.n_row, flat % self.n_col)

    def dev(self, x=None, z=None, y=None, k=None):
        x = self.x if x is None else x
        z = self.z if z is None else z
        y = self.y if y is None else y
        k = self.k if k is None else k
        return (x, z, y * 2 + k)

    def greet(self):
        sem = pltpu.get_barrier_semaphore()

        def one(i, carry):
            pl.semaphore_signal(
                sem, inc=1, device_id=self.of_flat((self.flat + i) % self.n), device_id_type=MESH
            )
            return carry

        lax.fori_loop(1, self.n, one, 0)

    def met(self):
        pl.semaphore_wait(pltpu.get_barrier_semaphore(), self.n - 1)


class Lanes:
    def __init__(self, send_sems, recv_sems):
        self.send_sems, self.recv_sems, self.sent = send_sems, recv_sems, []
        self.used = [0, 0]

    def take(self, which, count):
        first = self.used[which]
        self.used[which] += count
        return first

    def copy(self, src, dst, device, s, r):
        return pltpu.make_async_remote_copy(
            src_ref=src, dst_ref=dst, send_sem=self.send_sems.at[s],
            recv_sem=self.recv_sems.at[r], device_id=device, device_id_type=MESH,
        )

    def send(self, make, held=None):
        self.copy(*make()).start()
        self.sent.append((make, held))

    def arrived(self, landing, device, r):
        self.copy(landing, landing, device, 0, r).wait_recv()

    def finish(self):
        for make, held in self.sent:
            if held is None:
                self.copy(*make()).wait_send()
            else:
                pl.when(held())(lambda make=make: self.copy(*make()).wait_send())
        self.sent = []


class Gather:
    def __init__(self, place, lanes, region, first):
        self.p, self.lanes, self.region, self.first = p, lanes, region, first = place, lanes, region, first
        self.to_x, self.to_y, self.to_core = p.dev(x=1 - p.x), p.dev(y=1 - p.y), p.dev(k=1 - p.k)
        self.one, self.two = (self.to_x, self.to_y) if first == "x" else (self.to_y, self.to_x)
        n = p.n_row
        self.s = {name: lanes.take(0, n) for name in ("up", "down", 1, 2, 3, "core")}
        self.r = {name: lanes.take(1, n) for name in ("z", 1, 2, 3, "core")}

    def side(self, hop):
        p = self.p
        x_side = hop in ((1, 3) if self.first == "x" else (2, 3))
        y_side = hop in ((2, 3) if self.first == "x" else (1, 3))
        return (1 - p.x if x_side else p.x), (1 - p.y if y_side else p.y)

    def at(self, hop, z, k):
        x, y = self.side(hop)
        return self.region(x, z, 1, y, k)

    def line(self, hop, k):
        x, y = self.side(hop)
        return self.region(x, 0, self.p.n_row, y, k)

    def start(self, own):
        p = self.p

        def to(hop, device):
            return lambda: (own, self.at(0, p.z, p.k), device, self.s[hop] + p.z, self.r[hop] + p.z)

        self.lanes.send(to(1, self.one))
        self.lanes.send(to(2, self.two))
        self.own = own

    def z_start(self):
        p, own = self.p, self.own
        for name, step in (("up", 1), ("down", -1)):
            def held(step=step):
                return p.z + 1 < p.n_row if step == 1 else p.z >= 1

            def make(name=name, step=step):
                return (own, self.at(0, p.z, p.k), p.dev(z=p.z + step), self.s[name] + p.z, self.r["z"] + p.z)

            pl.when(held())(lambda make=make, held=held: self.lanes.send(make, held))

    def z_step(self, distance):
        p = self.p
        for name, step in (("up", 1), ("down", -1)):
            source = (lambda step=step: p.z - step * distance)

            def here(step=step):
                return p.z >= distance if step == 1 else p.z + distance < p.n_row

            def further(step=step):
                if step == 1:
                    return (p.z >= distance) & (p.z + 1 < p.n_row)
                return (p.z + distance < p.n_row) & (p.z >= 1)

            def arrive(name=name, step=step, source=source):
                ref = self.at(0, source(), p.k)
                self.lanes.arrived(ref, p.dev(z=p.z - step), self.r["z"] + source())

            def onward(name=name, step=step, source=source):
                ref = self.at(0, source(), p.k)
                return (ref, ref, p.dev(z=p.z + step), self.s[name] + source(), self.r["z"] + source())

            def over(hop, device, source=source):
                def make():
                    ref = self.at(0, source(), p.k)
                    return (ref, ref, device, self.s[hop] + source(), self.r[hop] + source())
                return make

            def body():
                arrive()
                if distance < p.n_row - 1:
                    pl.when(further())(lambda: self.lanes.send(onward, further))
                self.lanes.send(over(1, self.one), here)
                self.lanes.send(over(2, self.two), here)

            pl.when(here())(body)

    def z_steps(self):
        for distance in range(1, self.p.n_row):
            self.z_step(distance)
        self.z_done()

    def z_done(self):
        self.local.wait()
        self.to_other_core(0)

    def to_other_core(self, hop):
        def make():
            line = self.line(hop, self.p.k)
            return (line, line, self.to_core, self.s["core"] + hop, self.r["core"] + hop)
        self.lanes.send(make)

    def first_steps(self):
        p = self.p
        n = p.n_row
        order = (lambda: p.z, lambda: p.z + 1 - 2 * (p.z % 2), lambda: n - 1 - p.z, lambda: (p.z + n // 2) % n)
        for source in order:
            self.lanes.arrived(self.at(1, source(), p.k), self.one, self.r[1] + source())

            def make(source=source):
                ref = self.at(1, source(), p.k)
                return (ref, ref, self.two, self.s[3] + source(), self.r[3] + source())

            self.lanes.send(make)
        self.to_other_core(1)

    def second_steps(self, hops=(2, 3)):
        p = self.p
        for hop in hops:
            for i in range(p.n_row):
                self.lanes.arrived(self.at(hop, i, p.k), self.two, self.r[hop] + i)
            self.to_other_core(hop)

    def stage(self, name):
        if name == "z":
            self.z_start()
        elif name == "f":
            self.first_steps()
        elif name == "s":
            self.second_steps((2,))
        elif name == "t":
            self.second_steps((3,))
        else:
            self.z_step(int(name))
            if int(name) == self.p.n_row - 1:
                self.z_done()

    def end(self):
        for hop in range(4):
            self.lanes.arrived(self.line(hop, 1 - self.p.k), self.to_core, self.r["core"] + hop)


def rows_region(ref, n_row, low=0, high=None):
    width = ref.shape[3] // 2
    high = width if high is None else high

    def region(x, z, nz, y, k):
        columns = pl.ds(aligned(y * width + low, 128), high - low)
        if nz == 1:
            return ref.at[x * n_row + z, k, :, columns]
        return ref.at[pl.ds(x * n_row + z, nz), k, :, columns]

    return region


def lanes_region(ref, n_dp, n_row, low=0, high=None):
    width = ref.shape[3] // (n_dp * n_row)
    high = ref.shape[2] if high is None else high

    def region(x, z, nz, y, k):
        return ref.at[y, k, pl.ds(low, high - low), pl.ds(aligned((x * n_row + z) * width, 128), nz * width)]

    return region


CHUNK = 512
ROWS = 256
BATCH = (6, 6, 6, 6, 7)
SCHEDULE = {
    "first": {4: "oz uz", 5: "o1 u1 vz"},
    "turn": {0: "o2 u2 v1 dz", 2: "o3 u3 v2 d1"},
    "project": {0: "of v3 d2", 3: "uf d3", 6: "vf ez"},
    "attend": {0: "df os e1", 1: "e2", 2: "us e3", 3: "ot ut", 4: "ef", 5: "vs", 6: "vt", 8: "cot", 9: "ds", 11: "dt"},
    "mix": {1: "es"},
    "rise": {0: "et"},
}


def forward_kernel(
    dims, seq_ref, len_ref, tok_ref, cot_ref, qkv_ref, out_ref, up_ref, down_ref, norm_ref,
    xt_out, wqkv_out, qkv_out, ctx_out, lse_out, output_out, gm_out, dctx_out, gout_out, gup_out, gdown_out, nsum_out,
    tsend, half_qkv, half_out, half_up, pair_qkv, pair_out, pair_up,
    xt_v, x_v, w_v, wide_v, ctx_v, lse_v, wout_v, wup_v, wdown_v, norm_v, gains_v, cot_v, act_v, mixed_v, gsum_v, hl_v,
    output_v, down_v, attn_v, dctx_v, turn_v, nsum_v,
    tok_send, tok_recv, norm_send, norm_recv, cot_send, cot_recv, w_send, w_recv, half_send, half_recv, local_sem, out_send, out_recv,
):
    n_dp, n_row, n_col = dims
    p = Place(n_dp, n_row, n_col)
    micro, slots, _, span = tok_ref.shape
    rows, width = x_v.shape
    qkv_v = wide_v.at[:, pl.ds(0, 3 * width)]
    p.greet()
    for m in range(micro):
        for j in range(slots):
            tsend[m * slots + j] = tok_ref[m, seq_ref[m, j]]
    p.met()
    halves = Lanes(half_send, half_recv)
    lanes = Lanes(w_send, w_recv)
    partner = p.dev(k=1 - p.k)
    for i, (block, landing) in enumerate(((qkv_ref, half_qkv), (out_ref, half_out), (up_ref, half_up))):
        def make(i=i, block=block, landing=landing):
            count = landing.shape[0]
            return (block.at[pl.ds(aligned((1 - p.k) * count, 16), count), :], landing, partner, i, i)
        halves.send(make)

    def join(i, block, landing, pair):
        halves.arrived(landing, partner, i)
        count, across = landing.shape
        mine = block[pl.ds(aligned(p.k * count, 16), count), :]
        theirs = landing[...]
        pair[:, :across] = jnp.where(p.k == 0, mine, theirs)
        pair[:, across:] = jnp.where(p.k == 0, theirs, mine)

    local = []

    def keep(src, dst):
        made = pltpu.make_async_copy(src, dst, local_sem.at[len(local)])
        made.start()
        local.append(made)
        return made

    region_qkv = rows_region(w_v, n_row)
    join(0, qkv_ref, half_qkv, pair_qkv)
    own_w = keep(pair_qkv, region_qkv(p.x, p.z, 1, p.y, p.k))
    g_qkv = Gather(p, lanes, region_qkv, "x")
    g_qkv.local = own_w
    g_qkv.start(pair_qkv)
    g_qkv.z_start()

    def tok_copy(i):
        target = (p.flat + i) % p.n
        return pltpu.make_async_remote_copy(
            src_ref=tsend.at[(target % n_col) * slots + target // n_col],
            dst_ref=xt_v.at[p.g, :, pl.ds(aligned(p.c * span, 128), span)],
            send_sem=tok_send.at[i], recv_sem=tok_recv.at[i],
            device_id=p.of_flat(target), device_id_type=MESH,
        )

    def norm_copy(i):
        return pltpu.make_async_remote_copy(
            src_ref=norm_ref, dst_ref=norm_v.at[p.flat],
            send_sem=norm_send.at[i], recv_sem=norm_recv.at[i],
            device_id=p.of_flat((p.flat + i) % p.n), device_id_type=MESH,
        )

    sent = [1]

    def tok_batch(count):
        def one(j, carry):
            tok_copy((j * 13) % p.n).start()
            return carry

        lax.fori_loop(sent[0], min(sent[0] + count, p.n), one, 0)
        sent[0] = min(sent[0] + count, p.n)

    def norm_start(i, carry):
        norm_copy(i).start()
        return carry

    tok_batch(BATCH[0])
    own_tok = keep(tsend.at[p.c * slots + p.g], xt_v.at[p.g, :, pl.ds(aligned(p.c * span, 128), span)])

    waves = []

    def wave(own, region, first):
        gather = Gather(p, lanes, region, first)
        gather.local = keep(own, region(p.x, p.z, 1, p.y, p.k))
        gather.start(own)
        waves.append(gather)

    join(1, out_ref, half_out, pair_out)
    wave(pair_out, rows_region(wout_v, n_row), "y")
    join(2, up_ref, half_up, pair_up)
    cut = pair_up.shape[1] // 2
    wave(pair_up.at[:, pl.ds(0, cut)], rows_region(wup_v, n_row, 0, cut), "y")
    wave(pair_up.at[:, pl.ds(cut, cut)], rows_region(wup_v, n_row, cut, 2 * cut), "y")
    cut = down_ref.shape[0] // 2
    wave(down_ref.at[pl.ds(0, cut), :], lanes_region(wdown_v, n_dp, n_row, 0, cut), "y")
    wave(down_ref.at[pl.ds(cut, cut), :], lanes_region(wdown_v, n_dp, n_row, cut, 2 * cut), "y")
    lax.fori_loop(1, p.n, norm_start, 0)
    own_norm = keep(norm_ref, norm_v.at[p.flat])

    def cot_copy(i):
        target = (p.c + i) % n_col
        return pltpu.make_async_remote_copy(
            src_ref=cot_ref.at[target], dst_ref=cot_v.at[p.c],
            send_sem=cot_send.at[i], recv_sem=cot_recv.at[i],
            device_id=(p.x, p.z, target), device_id_type=MESH,
        )

    own_cot = keep(cot_ref.at[p.c], cot_v.at[p.c])
    names = dict(zip("ouvde", waves))

    def begin_cot():
        for i in range(1, n_col):
            cot_copy(i).start()

    def agenda(phase):
        table = {}
        for turn, steps in SCHEDULE.get(phase, {}).items():
            table[turn] = [begin_cot if step == "cot" else functools.partial(names[step[0]].stage, step[1:]) for step in steps.split()]
        return table

    first = agenda("first")

    def now(turn):
        for act in first.get(turn, ()):
            act()

    now(0)
    for distance in range(1, n_row):
        g_qkv.z_step(distance)
        tok_batch(BATCH[distance])
        now(distance)
    g_qkv.z_done()
    g_qkv.first_steps()
    tok_batch(BATCH[4])
    now(4)
    g_qkv.second_steps()
    tok_batch(p.n)
    now(5)
    own_tok.wait()

    def tok_wait(i, carry):
        source = (p.flat + p.n - i) % p.n
        landing = xt_v.at[source // n_col, :, pl.ds(aligned((source % n_col) * span, 128), span)]
        pltpu.make_async_remote_copy(
            src_ref=landing, dst_ref=landing, send_sem=tok_send.at[i], recv_sem=tok_recv.at[i],
            device_id=p.of_flat(source), device_id_type=MESH,
        ).wait_recv()
        return carry

    lax.fori_loop(1, p.n, tok_wait, 0)
    keep(xt_v, xt_out)

    def turn(i, carry):
        run_events(i, agenda("turn"))
        at = pl.ds(aligned(i * 256, 256), 256)
        x_v[at, :] = xt_v[:, :, at].reshape(width, 256).T
        return carry

    lax.fori_loop(0, rows // 256, turn, 0)
    g_qkv.end()
    keep(w_v, wqkv_out)

    def project(i, carry):
        run_events(i, agenda("project"))
        at = pl.ds(aligned(i * 256, 256), 256)
        wide_v[:, at] = product(x_v[...], w_v[:, :, :, at].reshape(width, 256)).astype(BF)
        return carry

    lax.fori_loop(0, 3 * width // 256, project, 0)
    kept_qkv = keep(qkv_v, qkv_out)
    out, up_a, up_b, down_a, down_b = waves
    length = len_ref[p.c, seq_ref[p.c, p.g]]
    bias = jnp.where(lax.broadcasted_iota(jnp.int32, (rows, 1), 0) < length, 0.0, NEGATIVE)
    chunks = rows // CHUNK

    def attend(step, carry):
        run_events(step, agenda("attend"))
        pair, at_row = step // chunks, step % chunks
        columns = [pl.ds(aligned(i * width + pair * 128, 128), 128) for i in range(3)]
        keys = wide_v[:, columns[1]]
        values_t = wide_v[:, columns[2]].T
        lane = lax.broadcasted_iota(jnp.int32, (rows, 128), 1)
        own_rows = pl.ds(aligned(at_row * CHUNK, CHUNK), CHUNK)
        queries = wide_v[own_rows, columns[0]] * jnp.asarray(0.125, BF)
        for h in range(2):
            mine = jnp.where((lane < HEAD) == (h == 0), keys, jnp.zeros_like(keys))
            scores = product_nt(mine, queries) + bias
            top = jnp.max(scores, axis=0, keepdims=True)
            exps = jnp.exp(scores - top)
            total = jnp.sum(exps, axis=0, keepdims=True)
            context = product(values_t[h * HEAD:(h + 1) * HEAD], exps.astype(BF))
            head_rows = pl.ds(aligned(pair * 128 + h * HEAD, HEAD), HEAD)
            ctx_v[head_rows, own_rows] = (context * (1.0 / total)).astype(BF)
            lse_v[2 * pair + h, :, own_rows] = top + jnp.log(total)
        return carry

    lax.fori_loop(0, width // 128 * chunks, attend, 0)
    keep(ctx_v, ctx_out)
    keep(lse_v, lse_out)

    own_norm.wait()

    def norm_wait(i, carry):
        source = (p.flat + p.n - i) % p.n
        pltpu.make_async_remote_copy(
            src_ref=norm_ref, dst_ref=norm_v.at[source], send_sem=norm_send.at[i], recv_sem=norm_recv.at[i],
            device_id=p.of_flat(source), device_id_type=MESH,
        ).wait_recv()
        return carry

    lax.fori_loop(1, p.n, norm_wait, 0)
    each = width // p.n
    gains_v[...] = jnp.zeros_like(gains_v)
    for source in range(p.n):
        low = source * each // 128 * 128
        gains_v[:, low:low + 256] += norm_v[source].astype(F32)
    gain_one, shift_one, gain_two, shift_two = (gains_v[i:i + 1, :width] for i in range(4))

    def normal(values):
        centered = values - jnp.mean(values, axis=-1, keepdims=True)
        scale = lax.rsqrt(jnp.mean(centered * centered, axis=-1, keepdims=True) + EPSILON)
        return centered * scale, scale

    def normal_back(grad, unit, scale, gain):
        grad = grad * gain
        return scale * (grad - jnp.mean(grad, axis=-1, keepdims=True) - unit * jnp.mean(grad * unit, axis=-1, keepdims=True))

    nsum_v[...] = jnp.zeros_like(nsum_v)
    whole = lambda ref: ref[...].reshape(width, -1)
    out.end()

    def mix(step, carry):
        run_events(step, agenda("mix"))
        at = pl.ds(aligned(step * ROWS, ROWS), ROWS)
        mixed = x_v[at, :].astype(F32) + product_tn(ctx_v[:, at], whole(wout_v))
        mixed_v[at, :] = mixed
        unit, _ = normal(mixed)
        hl_v[at, :] = (unit * gain_one + shift_one).astype(BF)
        return carry

    lax.fori_loop(0, rows // ROWS, mix, 0)
    up_a.end()
    up_b.end()
    kept_qkv.wait()

    def rise(step, carry):
        run_events(step, agenda("rise"))
        at = pl.ds(aligned(step * 256, 256), 256)
        pre = product(hl_v[...], wup_v[:, :, :, at].reshape(width, 256))
        half = 0.5 * (1.0 + lax.erf(pre * ROOT_HALF))
        act_v[:, at] = (pre * half).astype(BF)
        wide_v[:, at] = (half + pre * jnp.exp(pre * pre * -0.5) * ROOT_TWO_PI).astype(BF)
        return carry

    lax.fori_loop(0, 4 * width // 256, rise, 0)
    down_a.end()
    down_b.end()
    for i in range(1, n_col):
        source = (p.c + n_col - i) % n_col
        pltpu.make_async_remote_copy(
            src_ref=cot_v.at[source], dst_ref=cot_v.at[source],
            send_sem=cot_send.at[i], recv_sem=cot_recv.at[i],
            device_id=(p.x, p.z, source), device_id_type=MESH,
        ).wait_recv()
    own_cot.wait()

    def out_copy(target):
        return pltpu.make_async_remote_copy(
            src_ref=output_v.at[pl.ds(aligned(target * span, 16), span), :], dst_ref=output_out.at[p.c],
            send_sem=out_send.at[target], recv_sem=out_recv.at[p.c],
            device_id=(p.x, p.z, target), device_id_type=MESH,
        )

    def fall(step, carry):
        at = pl.ds(aligned(step * ROWS, ROWS), ROWS)
        unit_one, _ = normal(mixed_v[at, :])
        summed = unit_one * gain_one + shift_one + product_nt(act_v[at, :], whole(wdown_v))
        unit, scale = normal(summed)
        output_v[at, :] = (unit * gain_two + shift_two).astype(BF)
        per = span // ROWS
        cot = cot_v[step // per, pl.ds(aligned(step % per * ROWS, ROWS), ROWS), :].astype(F32)
        nsum_v[2:3, :] += jnp.sum(cot * unit, axis=0, keepdims=True)
        nsum_v[3:4, :] += jnp.sum(cot, axis=0, keepdims=True)
        grad = normal_back(cot, unit, scale, gain_two)
        gsum_v[at, :] = grad
        down_v[at, :] = grad.astype(BF)
        turn_v[:, at] = grad.T.astype(BF)
        target = step // per

        @pl.when((step % per == per - 1) & (target != p.c))
        def _():
            out_copy(target).start()
        return carry

    lax.fori_loop(0, rows // ROWS, fall, 0)
    keep(output_v.at[pl.ds(aligned(p.c * span, 16), span), :], output_out.at[p.c])

    def rise_back(step, carry):
        at = pl.ds(aligned(step * 256, 256), 256)
        back = product(down_v[...], wdown_v[:, :, :, at].reshape(width, 256))
        wide_v[:, at] = (back * wide_v[:, at].astype(F32)).astype(BF)
        return carry

    lax.fori_loop(0, 4 * width // 256, rise_back, 0)
    lanes.finish()

    def grad_down(step, carry):
        at = pl.ds(aligned(step * 256, 256), 256)
        wdown_v[:, :, :, at] = product(turn_v[...], act_v[:, at]).astype(BF).reshape(wdown_v.shape[:3] + (256,))
        return carry

    lax.fori_loop(0, 4 * width // 256, grad_down, 0)
    keep(wdown_v, gdown_out)

    def mix_back(step, carry):
        at = pl.ds(aligned(step * ROWS, ROWS), ROWS)
        grad = gsum_v[at, :] + product_nt(wide_v[at, :], whole(wup_v))
        unit, scale = normal(mixed_v[at, :])
        nsum_v[0:1, :] += jnp.sum(grad * unit, axis=0, keepdims=True)
        nsum_v[1:2, :] += jnp.sum(grad, axis=0, keepdims=True)
        grad = normal_back(grad, unit, scale, gain_one)
        gsum_v[at, :] = grad
        low = grad.astype(BF)
        attn_v[at, :] = low
        dctx_v[at, :] = product_nt(low, whole(wout_v)).astype(BF)
        turn_v[:, at] = hl_v[at, :].T
        return carry

    lax.fori_loop(0, rows // ROWS, mix_back, 0)
    keep(gsum_v, gm_out)
    keep(dctx_v, dctx_out)
    keep(nsum_v, nsum_out)

    def grad_up(step, carry):
        at = pl.ds(aligned(step * 256, 256), 256)
        wup_v[:, :, :, at] = product(turn_v[...], wide_v[:, at]).astype(BF).reshape(wup_v.shape[:3] + (256,))
        return carry

    lax.fori_loop(0, 4 * width // 256, grad_up, 0)
    keep(wup_v, gup_out)

    def grad_out(step, carry):
        at = pl.ds(aligned(step * 256, 256), 256)
        wout_v[:, :, :, at] = product(ctx_v[...], attn_v[:, at]).astype(BF).reshape(wout_v.shape[:3] + (256,))
        return carry

    lax.fori_loop(0, width // 256, grad_out, 0)
    keep(wout_v, gout_out)

    def small_wait(i, carry):
        norm_copy(i).wait_send()
        tok_copy(i).wait_send()
        return carry

    lax.fori_loop(1, p.n, small_wait, 0)
    for i in range(1, n_col):
        cot_copy(i).wait_send()
        source = (p.c + n_col - i) % n_col
        pltpu.make_async_remote_copy(
            src_ref=output_out.at[source], dst_ref=output_out.at[source],
            send_sem=out_send.at[source], recv_sem=out_recv.at[source],
            device_id=(p.x, p.z, source), device_id_type=MESH,
        ).wait_recv()
        out_copy((p.c + i) % n_col).wait_send()
    waited = [own_tok, own_norm, own_w, own_cot, kept_qkv] + [gather.local for gather in waves]
    for made in local:
        if not any(made is w for w in waited):
            made.wait()
    halves.finish()


def run_events(step, events):
    for when_, acts in events.items():
        def act(acts=acts):
            for a in acts:
                a()
        pl.when(step == when_)(act)


def forward(dims, seq_order, lengths, tok_t, cot, w_qkv, w_out, w_up, w_down_t, norms):
    n_dp, n_row, n_col = dims
    groups, n = n_dp * n_row, n_dp * n_row * n_col
    micro, slots, feats, span = tok_t.shape
    rows, width = n_col * span, groups * feats
    heads = width // HEAD
    qr, qc = w_qkv.shape
    orow, oc = w_out.shape
    ur, uc = w_up.shape
    dr, dc = w_down_t.shape
    shape = jax.ShapeDtypeStruct
    joined = (groups, 2, qr // 2, qc * n_col)
    out_all = (groups, 2, orow // 2, oc * n_col)
    up_all = (groups, 2, ur // 2, uc * n_col)
    down_all = (2, 2, dr, dc * groups)
    outs = (
        shape((groups, feats, rows), BF),
        shape(joined, BF),
        shape((rows, 3 * width), BF),
        shape((width, rows), BF),
        shape((heads, 1, rows), F32),
        shape((n_col, span, width), BF),
        shape((rows, width), F32),
        shape((rows, width), BF),
        shape(out_all, BF),
        shape(up_all, BF),
        shape(down_all, BF),
        shape((8, width), F32),
    )
    vm = pltpu.VMEM
    return pl.pallas_call(
        functools.partial(forward_kernel, dims),
        out_shape=outs,
        in_specs=[SM, SM, VM, ANY, VM, VM, VM, VM, VM],
        out_specs=[ANY] * len(outs),
        scratch_shapes=[
            vm((micro * slots, feats, span), BF),
            vm((qr // 2, qc), BF), vm((orow // 2, oc), BF), vm((ur // 2, uc), BF),
            vm((qr // 2, qc * 2), BF), vm((orow // 2, oc * 2), BF), vm((ur // 2, uc * 2), BF),
            vm((groups, feats, rows), BF),
            vm((rows, width), BF),
            vm(joined, BF),
            vm((rows, 4 * width), BF),
            vm((width, rows), BF),
            vm((heads, 1, rows), F32),
            vm(out_all, BF), vm(up_all, BF), vm(down_all, BF),
            vm((n,) + norms.shape, BF),
            vm((norms.shape[0], width + 256), F32),
            vm(cot.shape, BF),
            vm((rows, 4 * width), BF),
            vm((rows, width), F32), vm((rows, width), F32),
            vm((rows, width), BF), vm((rows, width), BF), vm((rows, width), BF), vm((rows, width), BF), vm((rows, width), BF),
            vm((width, rows), BF),
            vm((8, width), F32),
            DMA((n,)), DMA((n,)), DMA((n,)), DMA((n,)), DMA((n_col,)), DMA((n_col,)),
            DMA((6 * 6 * n_row,)), DMA((6 * 5 * n_row,)), DMA((3,)), DMA((3,)), DMA((24,)), DMA((n_col,)), DMA((n_col,)),
        ],
        compiler_params=pltpu.CompilerParams(
            collective_id=0, has_side_effects=True, vmem_limit_bytes=63 * 2**20
        ),
        name="forward_part",
    )(seq_order, lengths, tok_t, cot, w_qkv, w_out, w_up, w_down_t, norms)


BACK_CHUNK = 256


def add_into(target, term):
    shape = target.shape
    if len(shape) == 2:
        target[...] = (target[...].astype(F32) + term[...].astype(F32)).astype(BF)
        return

    def body(i, carry):
        target[i] = (target[i].astype(F32) + term[i].astype(F32)).astype(BF)
        return carry

    lax.fori_loop(0, shape[0], body, 0)


class Reduce:
    def __init__(self, place, lanes, theirs, mine, buffers, kind, first):
        self.p, self.lanes, self.theirs, self.mine, self.b = place, lanes, theirs, mine, buffers
        self.kind, self.axes = kind, ("x", "y") if first == "x" else ("y", "x")
        self.s = [lanes.take(0, 1) for _ in range(3)] + [lanes.take(0, place.n_row - 1)]
        self.r = [lanes.take(1, 1) for _ in range(3)] + [lanes.take(1, place.n_row - 1)]

    def start(self):
        p = self.p
        self.lanes.send(lambda: (self.theirs, self.b[0], p.dev(k=1 - p.k), self.s[0], self.r[0]))

    def half(self, ref, axis, side):
        if self.kind == "lanes" and axis == "y":
            return ref.at[side]
        if self.kind == "rows" and axis == "x":
            count = ref.shape[0] // 2
            return ref.at[pl.ds(side * count, count)]
        width = ref.shape[-1] // 2
        lead = (slice(None),) * (len(ref.shape) - 1)
        return ref.at[lead + (pl.ds(aligned(side * width, 128), width),)]

    def where(self, axis):
        p = self.p
        return (p.x, p.dev(x=1 - p.x)) if axis == "x" else (p.y, p.dev(y=1 - p.y))

    def send_half(self, stage):
        def make():
            side, peer = self.where(self.axes[stage - 1])
            return (self.half(self.b[stage - 1], self.axes[stage - 1], 1 - side), self.b[stage], peer, self.s[stage], self.r[stage])

        self.lanes.send(make)

    def add_half(self, stage):
        side, peer = self.where(self.axes[stage - 1])
        self.lanes.arrived(self.b[stage], peer, self.r[stage])
        add_into(self.b[stage], self.half(self.b[stage - 1], self.axes[stage - 1], side))

    def one(self):
        p = self.p
        self.lanes.arrived(self.b[0], p.dev(k=1 - p.k), self.r[0])
        add_into(self.b[0], self.mine)
        self.send_half(1)

    def two(self):
        self.add_half(1)
        self.send_half(2)

    def part(self, z):
        ref = self.b[2]
        if self.kind == "rows":
            return ref.at[z]
        width = self.b[3].shape[-1]
        return ref.at[:, pl.ds(aligned(z * width, 128), width)]

    def three(self):
        p = self.p
        self.add_half(2)
        for i in range(1, p.n_row):
            def make(i=i):
                target = (p.z + i) % p.n_row
                return (self.part(target), self.b[3].at[i - 1], p.dev(z=target), self.s[3] + i - 1, self.r[3] + i - 1)
            self.lanes.send(make)

    def four(self):
        p = self.p
        total = self.part(p.z)[...].astype(F32)
        for i in range(1, p.n_row):
            source = (p.z + p.n_row - i) % p.n_row
            self.lanes.arrived(self.b[3].at[i - 1], p.dev(z=source), self.r[3] + i - 1)
            total = total + self.b[3][i - 1].astype(F32)
        return total


def piece_buffers(kind, first, lead, rows, columns, n_row, groups):
    if kind == "lanes":
        one = (2, rows, columns // 2) if first == "x" else (rows, columns)
        return [(2, rows, columns), one, (rows, columns // 2), (n_row - 1, rows, columns // groups)]
    one = (lead // 2, rows, columns) if first == "x" else (lead, rows, columns // 2)
    return [(lead, rows, columns), one, (lead // 2, rows, columns // 2), (n_row - 1, rows, columns // 2)]


def backward_kernel(
    dims, plan, seq_ref, qkv_ref, ctx_ref, lse_ref, dctx_ref, xt_ref, w_ref, gm_ref, gout_ref, gup_ref, gdown_ref,
    ngrad_ref, tgrad_ref, rqkv_ref, rout_ref, rup_ref, rdown_ref, nsum_ref, *scratch,
):
    n_dp, n_row, n_col = dims
    p = Place(n_dp, n_row, n_col)
    groups = n_dp * n_row
    (
        qkv_v, ctx_v, lse_v, dctx_v, xt_v, w_v, gm_v, m_out, m_up, m_down, grad_v, dqt_v, dk_v, dv_v, acc_k, acc_v, dxt_v, trecv,
        nrecv, fq, fo, fu, tok_send, tok_recv, norm_send, norm_recv, w_send, w_recv, local_sem,
    ) = scratch[:29]
    pieces = scratch[29:]
    micro, slots, _, span = tgrad_ref.shape
    width, rows = ctx_ref.shape
    p.greet()
    local = []

    def keep(src, dst):
        made = pltpu.make_async_copy(src, dst, local_sem.at[len(local)])
        made.start()
        local.append(made)
        return made

    needed = [keep(qkv_ref, qkv_v), keep(dctx_ref, dctx_v), keep(ctx_ref, ctx_v), keep(lse_ref, lse_v)]
    mine_down = keep(gdown_ref.at[:, p.k], m_down)
    mine_up = keep(gup_ref.at[:, p.k], m_up)
    mine_out = keep(gout_ref.at[:, p.k], m_out)
    later = [keep(w_ref, w_v), keep(gm_ref, gm_v), keep(xt_ref, xt_v)]
    p.met()
    lanes = Lanes(w_send, w_recv)
    partner = p.dev(k=1 - p.k)
    waves = {"down": [], "up": [], "out": [], "qkv": []}
    whole = {"down": gdown_ref, "up": gup_ref, "out": gout_ref, "qkv": grad_v}
    carried = {"down": m_down, "up": m_up, "out": m_out}
    for index, (name, kind, first, low, count) in enumerate(plan):
        at = pl.ds(low, count)
        theirs = whole[name].at[:, 1 - p.k, at]
        mine = carried[name].at[:, at] if name != "qkv" else grad_v.at[:, p.k, at]
        waves[name].append(Reduce(p, lanes, theirs, mine, pieces[4 * index:4 * index + 4], kind, first))
    d, u, o, q = waves["down"], waves["up"], waves["out"], waves["qkv"]

    def norm_copy(i):
        target = (p.flat + i) % p.n
        return pltpu.make_async_remote_copy(
            src_ref=ngrad_ref.at[target], dst_ref=nrecv.at[p.flat],
            send_sem=norm_send.at[i], recv_sem=norm_recv.at[i],
            device_id=p.of_flat(target), device_id_type=MESH,
        )

    def norm_start(i, carry):
        norm_copy(i).start()
        return carry

    d[0].start()
    u[0].start()
    lax.fori_loop(1, p.n, norm_start, 0)
    nrecv[p.flat] = ngrad_ref[p.flat]
    for made in needed:
        made.wait()
    mine_down.wait()
    mine_up.wait()
    mine_out.wait()

    def finish_rows(piece, temp, result, low):
        total = piece.four()
        count, across = total.shape[0], total.shape[1] // 2
        half_rows = result.shape[0] // 2
        temp[pl.ds(low, count), :] = jnp.where(p.k == 0, total[:, across:], total[:, :across])
        result[pl.ds(aligned(p.k * half_rows + low, 16), count), :] = jnp.where(p.k == 0, total[:, :across], total[:, across:])
        s, r = lanes.take(0, 1), lanes.take(1, 1)
        place = lambda k: result.at[pl.ds(aligned(k * half_rows + low, 16), count), :]
        lanes.send(lambda: (temp.at[pl.ds(low, count), :], place(p.k), partner, s, r))
        ends.append(lambda: lanes.arrived(place(1 - p.k), partner, r))

    ends = []

    def finish_down(piece, low):
        total = piece.four()
        rdown_ref[pl.ds(low, total.shape[0]), :] = total

    lows = {name: [low for other, _, _, low, _ in plan if other == name] for name in waves}
    down_end = [functools.partial(finish_down, piece, low) for piece, low in zip(d, lows["down"])]
    up_end = [functools.partial(finish_rows, piece, fu, rup_ref, low) for piece, low in zip(u, lows["up"])]
    out_end = [functools.partial(finish_rows, piece, fo, rout_ref, low) for piece, low in zip(o, lows["out"])]
    qkv_end = [functools.partial(finish_rows, piece, fq, rqkv_ref, low) for piece, low in zip(q, lows["qkv"])]
    events = {
        0: (d[1].start, u[1].start),
        1: (d[0].one, u[0].one),
        2: (d[2].start, u[2].start, o[0].start),
        4: (d[1].one,),
        5: (u[1].one,),
        6: (d[0].two,),
        7: (u[0].two,),
        9: (d[2].one,),
        10: (u[2].one,),
        11: (d[1].two,),
        12: (u[1].two, d[0].three),
        13: (u[0].three, o[0].one),
        15: (d[2].two,),
        16: (u[2].two, d[1].three),
        17: (u[1].three,),
        18: (o[0].two, down_end[0]),
        19: (up_end[0],),
        20: (d[2].three,),
        21: (u[2].three, o[0].three),
        22: (down_end[1],),
        23: (up_end[1],),
    }
    length_bias = jnp.where(lax.broadcasted_iota(jnp.int32, (rows, 1), 0) < seq_ref[1, p.c, seq_ref[0, p.c, p.g]], 0.0, NEGATIVE)
    chunks = rows // BACK_CHUNK

    def attend(step, carry):
        for when_, acts in events.items():
            def act(acts=acts):
                for a in acts:
                    a()
            pl.when(step == when_)(act)
        pair, at_row = step // chunks, step % chunks
        columns = [pl.ds(aligned(i * width + pair * 128, 128), 128) for i in range(3)]
        keys, values = qkv_v[:, columns[1]], qkv_v[:, columns[2]]
        keys_t = keys.T
        lane = lax.broadcasted_iota(jnp.int32, (rows, 128), 1)
        short = lax.broadcasted_iota(jnp.int32, (BACK_CHUNK, 128), 1)
        own_rows = pl.ds(aligned(at_row * BACK_CHUNK, BACK_CHUNK), BACK_CHUNK)
        queries = qkv_v[own_rows, columns[0]] * jnp.asarray(0.125, BF)
        back = dctx_v[own_rows, columns[0]]
        back_t = back.T.astype(F32)
        forth_t = ctx_v[pl.ds(aligned(pair * 128, 128), 128), own_rows].astype(F32)
        both = back_t * forth_t
        d_keys = d_values = None
        for h in range(2):
            def own(block, index):
                return jnp.where((index < HEAD) == (h == 0), block, jnp.zeros_like(block))
            delta = jnp.sum(both[h * HEAD:(h + 1) * HEAD], axis=0, keepdims=True)
            scores = product_nt(own(keys, lane), queries) + length_bias
            soft = jnp.exp(scores - lse_v[2 * pair + h, :, own_rows])
            d_probs = product_nt(own(values, lane), back)
            d_scores = (soft * (d_probs - delta)).astype(BF)
            head_rows = pl.ds(aligned(pair * 128 + h * HEAD, HEAD), HEAD)
            dqt_v[head_rows, own_rows] = (product(keys_t[h * HEAD:(h + 1) * HEAD], d_scores) * 0.125).astype(BF)
            to_values = product(soft.astype(BF), own(back, short))
            to_keys = product(d_scores, own(queries, short))
            d_values = to_values if d_values is None else d_values + to_values
            d_keys = to_keys if d_keys is None else d_keys + to_keys

        @pl.when(at_row == 0)
        def _():
            acc_k[...] = d_keys
            acc_v[...] = d_values

        @pl.when(at_row > 0)
        def _():
            acc_k[...] += d_keys
            acc_v[...] += d_values

        @pl.when(at_row == chunks - 1)
        def _():
            dk_v[:, columns[0]] = acc_k[...].astype(BF)
            dv_v[:, columns[0]] = acc_v[...].astype(BF)
        return carry

    lax.fori_loop(0, width // 128 * chunks, attend, 0)
    for made in later:
        made.wait()

    def tok_copy(target):
        return pltpu.make_async_remote_copy(
            src_ref=dxt_v.at[target // n_col, :, pl.ds(aligned((target % n_col) * span, 128), span)],
            dst_ref=trecv.at[p.c * slots + p.g],
            send_sem=tok_send.at[target], recv_sem=tok_recv.at[p.flat],
            device_id=p.of_flat(target), device_id_type=MESH,
        )

    half_groups = groups // 2
    half_width = width // 2
    for part in range(2):
        near = pl.ds(part * half_groups, half_groups)
        w_rows = lambda i: w_v[near, :, :, i * width:(i + 1) * width].reshape(half_width, width)
        total = gm_v[:, part * half_width:(part + 1) * half_width].T
        total = total + product(w_rows(0), dqt_v[...])
        total = total + product_nt(w_rows(1), dk_v[...])
        total = total + product_nt(w_rows(2), dv_v[...])
        dxt_v[near] = total.astype(BF).reshape(half_groups, width // groups, rows)

        def tok_start(i, carry, part=part):
            base = part * half_groups * n_col
            target = base + (p.flat + i) % (half_groups * n_col)

            @pl.when(target != p.flat)
            def _():
                tok_copy(target).start()
            return carry

        lax.fori_loop(0, half_groups * n_col, tok_start, 0)
    own_tok = keep(dxt_v.at[p.g, :, pl.ds(aligned(p.c * span, 128), span)], trecv.at[p.c * slots + p.g])

    def grad_q(i, carry):
        at = pl.ds(aligned(i * 256, 256), 256)
        grad_v[:, :, :, at] = product_nt(xt_v[...].reshape(width, rows), dqt_v[at, :]).astype(BF).reshape(groups, 2, -1, 256)
        return carry

    def grad_k(i, carry):
        at = pl.ds(aligned(i * 256, 256), 256)
        to = lambda j: pl.ds(aligned(j * width + i * 256, 256), 256)
        xt = xt_v[...].reshape(width, rows)
        grad_v[:, :, :, to(1)] = product(xt, dk_v[:, at]).astype(BF).reshape(groups, 2, -1, 256)
        grad_v[:, :, :, to(2)] = product(xt, dv_v[:, at]).astype(BF).reshape(groups, 2, -1, 256)
        return carry

    lax.fori_loop(0, width // 256, grad_q, 0)
    lax.fori_loop(0, width // 256, grad_k, 0)
    for piece in q:
        piece.start()
    for piece in q:
        piece.one()
    down_end[2]()
    up_end[2]()
    out_end[0]()
    for piece in q:
        piece.two()
    for piece in q:
        piece.three()

    def norm_wait(i, carry):
        source = (p.flat + p.n - i) % p.n
        pltpu.make_async_remote_copy(
            src_ref=nrecv.at[source], dst_ref=nrecv.at[source], send_sem=norm_send.at[i], recv_sem=norm_recv.at[i],
            device_id=p.of_flat(source), device_id_type=MESH,
        ).wait_recv()
        norm_copy(i).wait_send()
        return carry

    lax.fori_loop(1, p.n, norm_wait, 0)
    nsum_ref[...] = jnp.sum(nrecv[...], axis=0)
    for end in qkv_end:
        end()
    own_tok.wait()

    def tok_wait(i, carry):
        source = (p.flat + p.n - i) % p.n
        landing = trecv.at[(source % n_col) * slots + source // n_col]
        pltpu.make_async_remote_copy(
            src_ref=landing, dst_ref=landing, send_sem=tok_send.at[source], recv_sem=tok_recv.at[source],
            device_id=p.of_flat(source), device_id_type=MESH,
        ).wait_recv()
        tok_copy((p.flat + i) % p.n).wait_send()
        return carry

    lax.fori_loop(1, p.n, tok_wait, 0)
    for m in range(micro):
        for s in range(slots):
            place = jnp.int32(0)
            for j in range(slots):
                place = jnp.where(seq_ref[0, m, j] == s, jnp.int32(j), place)
            tgrad_ref[m, s] = trecv[m * slots + place]
    for end in ends:
        end()
    lanes.finish()


def backward(dims, seq_order, lengths, qkv, ctx_t, lse, d_context, xt, w_qkv, g_mixed, g_out, g_up, g_down_t, n_grads):
    n_dp, n_row, n_col = dims
    groups, n = n_dp * n_row, n_dp * n_row * n_col
    micro, slots = seq_order.shape
    width, rows = ctx_t.shape
    feats, span = width // groups, rows // n_col
    shape = jax.ShapeDtypeStruct
    plan, buffers = [], []
    for name, grad, kind, first, count in (
        ("down", g_down_t, "lanes", "x", 3), ("up", g_up, "rows", "y", 3), ("out", g_out, "rows", "x", 1),
        ("qkv", w_qkv, "rows", "y", 3),
    ):
        lead, _, across, columns = grad.shape
        each = across // count
        for i in range(count):
            plan.append((name, kind, first, i * each, each))
            buffers += [pltpu.VMEM(b, BF) for b in piece_buffers(kind, first, lead, each, columns, n_row, groups)]
    outs = (
        shape((micro, slots, feats, span), BF),
        shape((w_qkv.shape[2] * 2, w_qkv.shape[3] // n_col), F32),
        shape((g_out.shape[2] * 2, g_out.shape[3] // n_col), F32),
        shape((g_up.shape[2] * 2, g_up.shape[3] // n_col), F32),
        shape((g_down_t.shape[2], g_down_t.shape[3] // groups), F32),
        shape(n_grads.shape[1:], F32),
    )
    vm = lambda like, kind=BF: pltpu.VMEM(like.shape, kind)
    temps = [pltpu.VMEM((g.shape[2], g.shape[3] // n_col), F32) for g in (w_qkv, g_out, g_up)]
    carried = [pltpu.VMEM((g.shape[0],) + g.shape[2:], BF) for g in (g_out, g_up, g_down_t)]
    return pl.pallas_call(
        functools.partial(backward_kernel, dims, plan),
        out_shape=outs,
        in_specs=[SM, ANY, ANY, ANY, ANY, ANY, ANY, ANY, ANY, ANY, ANY, VM],
        out_specs=[VM, VM, VM, VM, VM, VM],
        scratch_shapes=[
            vm(qkv), vm(ctx_t), vm(lse, F32), vm(d_context), vm(xt), vm(w_qkv), vm(g_mixed, F32), *carried, vm(w_qkv),
            pltpu.VMEM((width, rows), BF), pltpu.VMEM((rows, width), BF), pltpu.VMEM((rows, width), BF),
            pltpu.VMEM((rows, 128), F32), pltpu.VMEM((rows, 128), F32),
            pltpu.VMEM((groups, feats, rows), BF), pltpu.VMEM((micro * slots, feats, span), BF),
            vm(n_grads, F32), *temps,
            DMA((n,)), DMA((n,)), DMA((n,)), DMA((n,)),
            DMA((80,)), DMA((80,)), DMA((16,)), *buffers,
        ],
        compiler_params=pltpu.CompilerParams(
            collective_id=1, has_side_effects=True, vmem_limit_bytes=62 * 2**20
        ),
        name="backward_part",
    )(jnp.stack([seq_order, lengths]), qkv, ctx_t, lse, d_context, xt, w_qkv, g_mixed, g_out, g_up, g_down_t, n_grads)
def layer_norm(values, factor, offset):
    average = jnp.mean(values, axis=-1, keepdims=True)
    centered = values - average
    variance = jnp.mean(centered * centered, axis=-1, keepdims=True)
    return centered * lax.rsqrt(variance + EPSILON) * factor + offset


def gelu_act(values):
    return 0.5 * values * (1.0 + lax.erf(values * ROOT_HALF))


def attention(qkv, length):
    rows, width = qkv.shape[0], qkv.shape[1] // 3
    heads = width // HEAD
    q, k, v = (qkv[:, i * width:(i + 1) * width].reshape(rows, heads, HEAD) for i in range(3))
    scores = jnp.einsum("qhe,khe->hqk", q, k, preferred_element_type=F32) * 0.125
    valid = jnp.arange(rows, dtype=jnp.int32) < length
    scores = jnp.where(valid[None, None, :], scores, NEGATIVE)
    top = jnp.max(scores, axis=-1, keepdims=True)
    exps = jnp.exp(scores - top)
    total = jnp.sum(exps, axis=-1, keepdims=True)
    probs = (exps / total).astype(BF)
    context = jnp.einsum("hqk,khe->qhe", probs, v, preferred_element_type=F32)
    return context.astype(BF).reshape(rows, width), top + jnp.log(total)


def attention_back(qkv, length, stats, d_context):
    rows, width = qkv.shape[0], qkv.shape[1] // 3
    heads = width // HEAD
    q, k, v = (qkv[:, i * width:(i + 1) * width].reshape(rows, heads, HEAD) for i in range(3))
    dc = d_context.reshape(rows, heads, HEAD)
    scores = jnp.einsum("qhe,khe->hqk", q, k, preferred_element_type=F32) * 0.125
    valid = jnp.arange(rows, dtype=jnp.int32) < length
    scores = jnp.where(valid[None, None, :], scores, NEGATIVE)
    soft = jnp.exp(scores - stats)
    d_probs = jnp.einsum("qhe,khe->hqk", dc, v, preferred_element_type=F32)
    delta = jnp.sum(soft * d_probs, axis=-1, keepdims=True)
    d_scores = (soft * (d_probs - delta)).astype(BF)
    dq = jnp.einsum("hqk,khe->qhe", d_scores, k, preferred_element_type=F32) * 0.125
    dk = jnp.einsum("hqk,qhe->khe", d_scores, q, preferred_element_type=F32) * 0.125
    dv = jnp.einsum("hqk,qhe->khe", soft.astype(BF), dc, preferred_element_type=F32)
    return jnp.concatenate([a.astype(BF).reshape(rows, width) for a in (dq, dk, dv)], axis=-1)


def middle(x, context, context_t, cot, w_out, w_up, w_down_t, gain_one, shift_one, gain_two, shift_two):
    mixed = x.astype(F32) + product(context, w_out)
    hidden = layer_norm(mixed, gain_one, shift_one)
    hidden_low = hidden.astype(BF)
    pre_act = product(hidden_low, w_up)
    act_low = gelu_act(pre_act).astype(BF)
    summed = hidden + product_nt(act_low, w_down_t)
    output = layer_norm(summed, gain_two, shift_two).astype(BF)
    _, norm_two_back = jax.vjp(layer_norm, summed, gain_two, shift_two)
    g_summed, g_gain_two, g_shift_two = norm_two_back(cot.astype(F32))
    d_down = g_summed.astype(BF)
    g_down_t = product_tn(d_down, act_low).astype(BF)
    d_act = product(d_down, w_down_t)
    _, gelu_back = jax.vjp(gelu_act, pre_act)
    d_pre = gelu_back(d_act)[0].astype(BF)
    g_up = product_tn(hidden_low, d_pre).astype(BF)
    g_hidden = g_summed + product_nt(d_pre, w_up)
    _, norm_one_back = jax.vjp(layer_norm, mixed, gain_one, shift_one)
    g_mixed, g_gain_one, g_shift_one = norm_one_back(g_hidden)
    d_attn = g_mixed.astype(BF)
    g_out = product(context_t, d_attn).astype(BF)
    d_context = product_nt(d_attn, w_out).astype(BF)
    return output, g_mixed, d_context, g_down_t, g_up, g_out, (g_gain_one, g_shift_one, g_gain_two, g_shift_two)


def take_blocks(blocks, places):
    def body(place_ref, in_ref, out_ref):
        def step(i, carry):
            out_ref[i] = in_ref[place_ref[i]]
            return carry

        lax.fori_loop(0, blocks.shape[0], step, 0)

    return pl.pallas_call(
        body, out_shape=jax.ShapeDtypeStruct(blocks.shape, blocks.dtype), in_specs=[SM, VM], out_specs=VM,
        compiler_params=pltpu.CompilerParams(vmem_limit_bytes=48 * 2**20), name="take_blocks",
    )(places, blocks)


def own_length(lengths, seq_order):
    n_row = lax.axis_size("row")
    slot = lax.axis_index("dp") * n_row + lax.axis_index("row")
    micro = lax.axis_index("col")
    index = jnp.arange(seq_order.shape[1], dtype=jnp.int32)
    order = jnp.sum(jnp.where(jnp.arange(seq_order.shape[0])[:, None] == micro, seq_order, 0), axis=0)
    source = jnp.sum(jnp.where(index == slot, order, 0))
    mine = jnp.sum(jnp.where(jnp.arange(seq_order.shape[0])[:, None] == micro, lengths, 0), axis=0)
    return jnp.sum(jnp.where(index == source, mine, 0))


def local(
    tokens, cotangent, lengths, seq_order, w_qkv, w_out, w_up, w_down, gain_one, shift_one, gain_two, shift_two,
):
    dims = tuple(lax.axis_size(a) for a in ("dp", "row", "col"))
    n_dp, n_row, n_col = dims
    groups = n_dp * n_row
    micro, slots, span, feats = tokens.shape
    width = cotangent.shape[3]
    rows = span * n_col
    direct = n_dp == 2 and n_col == 4 and feats % 32 == 0 and w_qkv.shape[0] % 32 == 0
    tok_t = jnp.swapaxes(tokens, 2, 3)
    w_down_t = w_down.T
    norms = jnp.stack([gain_one, shift_one, gain_two, shift_two])
    length = own_length(lengths, seq_order)
    everyone = ("dp", "row", "col")
    if direct:
        each = norms.shape[1]
        place = (lax.axis_index("dp") * n_row + lax.axis_index("row")) * n_col + lax.axis_index("col")
        lane = jnp.arange(256, dtype=jnp.int32)
        here = lane[None, :] == (place * each) % 128 + jnp.arange(each, dtype=jnp.int32)[:, None]
        packed = jnp.sum(jnp.where(here[None], norms[:, :, None].astype(F32), 0.0), axis=1).astype(BF)
        packed = jnp.pad(packed, ((0, 12), (0, 0)))
        xt, w_joined, qkv, context_t, lse, output, g_mixed, d_context, g_out, g_up, g_down_t, norm_grads = forward(
            dims, seq_order, lengths, tok_t, cotangent[:, 0], w_qkv, w_out, w_up, w_down_t, packed
        )
        norm_grads = norm_grads[:4]
    else:
        offset = jnp.arange(micro, dtype=jnp.int32)[:, None] * slots
        sent = take_blocks(tok_t.reshape(micro * slots, feats, span), (seq_order + offset).reshape(-1))
        sent = jnp.swapaxes(sent.reshape(micro, slots, feats, span), 0, 1).reshape(micro * slots, feats, span)
        got = lax.all_to_all(sent, everyone, split_axis=0, concat_axis=0, tiled=True)
        xt = got.reshape(groups, n_col, feats, span).transpose(0, 2, 1, 3).reshape(width, rows)
        cot = lax.all_to_all(cotangent[:, 0], "col", split_axis=0, concat_axis=0, tiled=True).reshape(rows, width)

        def whole(w, row_axes, col_axes):
            w = lax.all_gather(w, col_axes, axis=1, tiled=True)
            return lax.all_gather(w, row_axes, axis=0, tiled=True)

        f_qkv, f_out, f_up = (whole(w, ("dp", "row"), "col") for w in (w_qkv, w_out, w_up))
        f_down_t = whole(w_down_t, "col", ("dp", "row"))
        f_norms = lax.all_gather(norms, everyone, axis=1, tiled=True)
    if direct:
        n_grads = jnp.swapaxes(norm_grads.reshape(4, width // each, each), 0, 1)
        n_grads = jnp.pad(n_grads, ((0, 0), (0, 4), (0, 128 - each)))
        tgrad, r_qkv, r_out, r_up, r_down_t, n_sum = backward(
            dims, seq_order, lengths, qkv, context_t, lse, d_context, xt, w_joined, g_mixed,
            g_out, g_up, g_down_t, n_grads,
        )
        n_sum = n_sum[:4, :each]
    else:
        gains = [f_norms[i].astype(F32) for i in range(4)]
        x = xt.T
        qkv = product(x, f_qkv).astype(BF)
        context, stats = attention(qkv, length)
        output, g_mixed, d_context, g_down_t, g_up, g_out, norm_grads = middle(
            x, context, context.T, cot, f_out, f_up, f_down_t, *gains
        )
        norm_grads = jnp.stack(norm_grads)
        d_qkv = attention_back(qkv, length, stats, d_context)
        g_qkv = product(xt, d_qkv).astype(BF)
        dxt = (g_mixed + product_nt(d_qkv, f_qkv)).astype(BF).T
        n_sum = lax.psum_scatter(norm_grads, everyone, scatter_dimension=1, tiled=True)
        output = lax.all_to_all(output.reshape(n_col, span, width), "col", split_axis=0, concat_axis=0, tiled=True)
        sent = dxt.reshape(groups, feats, n_col, span).transpose(0, 2, 1, 3).reshape(micro * slots, feats, span)
        got = lax.all_to_all(sent, everyone, split_axis=0, concat_axis=0, tiled=True)
        got = jnp.swapaxes(got.reshape(slots, micro, feats, span), 0, 1).reshape(micro * slots, feats, span)
        index = jnp.arange(slots, dtype=jnp.int32)
        inverse = jnp.sum(jnp.where(seq_order[:, :, None] == index, index[None, :, None], 0), axis=1)
        offset = jnp.arange(micro, dtype=jnp.int32)[:, None] * slots
        tgrad = take_blocks(got, (inverse + offset).reshape(-1)).reshape(micro, slots, feats, span)

        def parts(g, row_axes, col_axes):
            g = lax.psum_scatter(g, col_axes, scatter_dimension=1, tiled=True)
            return lax.psum_scatter(g, row_axes, scatter_dimension=0, tiled=True).astype(F32)

        r_qkv, r_out, r_up = (parts(g, ("dp", "row"), "col") for g in (g_qkv, g_out, g_up))
        r_down_t = parts(g_down_t, "col", ("dp", "row"))
    return (
        output[:, None], jnp.swapaxes(tgrad, 2, 3), r_qkv, r_out, r_up, r_down_t.T,
        n_sum[0], n_sum[1], n_sum[2], n_sum[3],
    )


def solution(mesh):
    rows = ("dp", "row")
    every = ("dp", "row", "col")
    in_specs = (
        P(None, None, "col", rows), P(None, rows, "col", None), P(), P(),
        P(rows, "col"), P(rows, "col"), P(rows, "col"), P(rows, "col"),
        P(every), P(every), P(every), P(every),
    )
    out_specs = (
        P(None, rows, "col", None), P(None, None, "col", rows),
        P(rows, "col"), P(rows, "col"), P(rows, "col"), P(rows, "col"),
        P(every), P(every), P(every), P(every),
    )
    return jax.shard_map(local, mesh=mesh, in_specs=in_specs, out_specs=out_specs, check_vma=False)
```

profile of v0, /device:TPU:0, one launch (start us, length us, event | category | flops | bytes accessed | tf_op | source)
XLA Modules:
  0.0 302.7 jit_solution(1259537703506575963)
XLA Ops:
  0.7 0.7 maximum_convert_fusion
  1.4 1.3 pad_add_fusion.seq_ref
  2.7 0.1 iota_compare_fusion
  2.8 0.1 select_reduce_fusion
  2.9 0.6 pad.8.norm_ref
  3.5 169.5 %forward_part.1 = (bf16[8,96,1024]{2,1,0:T(8,128)(2,1)}, bf16[8,2,48,2304]{3,2,1,0:T(8,128)(2,1)}, bf16[1024,2304]{1,0:T(8,128)(2,1)}, bf16[768,1024]{1,0:T(8,12...) custom-call(s32[4,8]{1,0:T(4,128)} %seq_ref.1, ...), custom_call_target="tpu_custom_call" | custom-call | tf_op jit(solution)/shard_map/forward_part/pallas_call | solution.py:694
  173.0 0.7 slice.20
  173.7 0.1 reshape.81
  173.9 0.7 pad.9.ngrad_ref
  174.5 0.0 copy-start
  174.5 120.9 %backward_part.1 = (bf16[4,8,96,256]{3,2,1,0:T(8,128)(2,1)}, f32[96,576]{1,0:T(8,128)}, f32[96,192]{1,0:T(8,128)}, f32[96,768]{1,0:T(8,128)}, f32[192,384]{1,0:T(8,128)}, /*index=5*/f32[8,128]{1,0:T(8,128)}) custom-call(s32[2,4,8]{2,1,0:T(4,128)} %pad_add_fusion.seq_ref, bf16[1024,2304]{1,0:T(8,128)(2,1)} %get-tuple-element.29.qkv_ref, ...), custom_call_target="tpu_custom_call" | custom-call | tf_op jit(solution)/shard_map/backward_part/pallas_call | solution.py:1113
  295.4 1.4 slice_bitcast_fusion
  296.8 0.0 copy-done
  296.8 0.0 copy-start.1
  296.8 1.1 copy.35
  298.0 0.8 copy-done.1
  298.8 0.0 copy-start.4
  298.8 0.0 copy-start.5
  298.8 0.0 copy-start.3
  298.8 0.0 copy-start.2
  298.8 1.1 copy.36
  299.9 0.0 copy-done.4
  299.9 0.7 copy.37
  300.6 0.0 copy-done.5
  300.6 0.6 copy.38
  301.3 0.0 copy-done.3
  301.3 0.7 copy.39
  302.0 0.0 copy-done.2
  302.0 0.7 copy.40
  (2 shorter events, 0.0 us)
Async XLA Ops:
  174.5 122.3 %copy-start = (bf16[4,256,768]{2,1,0:T(8,128)(2,1)S(1)}, bf16[4,256,768]{2,1,0:T(8,128)(2,1)}, u32[]{:S(2)}) copy-start(bf16[4,256,768]{2,1,0:T(8,128)(2,1)} %get-tuple-element.28) | copy-start | bytes 4718596
  296.8 2.0 copy-start.1
  298.8 1.2 copy-start.4
  298.8 1.9 copy-start.5
  298.8 2.5 copy-start.3
  298.8 3.2 %copy-start.2 = (f32[192,384]{1,0:T(8,128)S(1)}, f32[192,384]{1,0:T(8,128)}, u32[]{:S(2)}) copy-start(f32[192,384]{1,0:T(8,128)} %get-tuple-element.44) | copy-start | bytes 884740
where the time goes:
time: 304 us; the launch traced here: 303 us
  Pallas kernels  290 us (95%)
  local copies, waits for them, and re-layouts  9.41 us (3%)
    pallas_call x1, Pallas kernels, forward(): pl.pallas_call(functools.partial(forward_kernel, dims), out_shape=outs, i...  170 us
    pallas_call x1, Pallas kernels, backward(): pl.pallas_call(functools.partial(backward_kernel, dims, plan), out_shape=...  121 us

commit v1 on v0

--- a/solution.py
+++ b/solution.py
@@ -90,19 +90,16 @@
             recv_sem=self.recv_sems.at[r], device_id=device, device_id_type=MESH,
         )
 
-    def send(self, make, held=None):
+    def send(self, make):
         self.copy(*make()).start()
-        self.sent.append((make, held))
+        self.sent.append(make)
 
     def arrived(self, landing, device, r):
         self.copy(landing, landing, device, 0, r).wait_recv()
 
     def finish(self):
-        for make, held in self.sent:
-            if held is None:
-                self.copy(*make()).wait_send()
-            else:
-                pl.when(held())(lambda make=make: self.copy(*make()).wait_send())
+        for make in self.sent:
+            self.copy(*make()).wait_send()
         self.sent = []
 
 
@@ -112,8 +109,12 @@
         self.to_x, self.to_y, self.to_core = p.dev(x=1 - p.x), p.dev(y=1 - p.y), p.dev(k=1 - p.k)
         self.one, self.two = (self.to_x, self.to_y) if first == "x" else (self.to_y, self.to_x)
         n = p.n_row
-        self.s = {name: lanes.take(0, n) for name in ("up", "down", 1, 2, 3, "core")}
+        self.s = {name: lanes.take(0, n) for name in ("z", 1, 2, 3, "core")}
         self.r = {name: lanes.take(1, n) for name in ("z", 1, 2, 3, "core")}
+        self.far = (p.z + n // 2) % n
+        self.near = p.z + 1 - 2 * (p.z % 2)
+        self.cross = (self.near + n // 2) % n
+        self.to_near = p.dev(z=self.near)
 
     def side(self, hop):
         p = self.p
@@ -141,50 +142,25 @@
 
     def z_start(self):
         p, own = self.p, self.own
-        for name, step in (("up", 1), ("down", -1)):
-            def held(step=step):
-                return p.z + 1 < p.n_row if step == 1 else p.z >= 1
-
-            def make(name=name, step=step):
-                return (own, self.at(0, p.z, p.k), p.dev(z=p.z + step), self.s[name] + p.z, self.r["z"] + p.z)
-
-            pl.when(held())(lambda make=make, held=held: self.lanes.send(make, held))
-
-    def z_step(self, distance):
+        self.lanes.send(lambda: (own, self.at(0, p.z, p.k), p.dev(z=self.far), self.s["z"], self.r["z"]))
+        self.lanes.send(lambda: (own, self.at(0, p.z, p.k), p.dev(z=self.near), self.s["z"] + 1, self.r["z"] + 1))
+
+    def z_step(self, number):
         p = self.p
-        for name, step in (("up", 1), ("down", -1)):
-            source = (lambda step=step: p.z - step * distance)
-
-            def here(step=step):
-                return p.z >= distance if step == 1 else p.z + distance < p.n_row
-
-            def further(step=step):
-                if step == 1:
-                    return (p.z >= distance) & (p.z + 1 < p.n_row)
-                return (p.z + distance < p.n_row) & (p.z >= 1)
-
-            def arrive(name=name, step=step, source=source):
-                ref = self.at(0, source(), p.k)
-                self.lanes.arrived(ref, p.dev(z=p.z - step), self.r["z"] + source())
-
-            def onward(name=name, step=step, source=source):
-                ref = self.at(0, source(), p.k)
-                return (ref, ref, p.dev(z=p.z + step), self.s[name] + source(), self.r["z"] + source())
-
-            def over(hop, device, source=source):
-                def make():
-                    ref = self.at(0, source(), p.k)
-                    return (ref, ref, device, self.s[hop] + source(), self.r[hop] + source())
-                return make
-
-            def body():
-                arrive()
-                if distance < p.n_row - 1:
-                    pl.when(further())(lambda: self.lanes.send(onward, further))
-                self.lanes.send(over(1, self.one), here)
-                self.lanes.send(over(2, self.two), here)
-
-            pl.when(here())(body)
+        source = (self.far, self.near, self.cross)[number - 1]
+        peer = self.far if number == 1 else self.near
+        self.lanes.arrived(self.at(0, source, p.k), p.dev(z=peer), self.r["z"] + number - 1)
+
+        def to(device, hop, index):
+            def make():
+                ref = self.at(0, source, p.k)
+                return (ref, ref, device, self.s[hop] + index, self.r[hop] + index)
+            return make
+
+        if number == 1:
+            self.lanes.send(to(self.to_near, "z", 2))
+        self.lanes.send(to(self.one, 1, source))
+        self.lanes.send(to(self.two, 2, source))
 
     def z_steps(self):
         for distance in range(1, self.p.n_row):
@@ -203,14 +179,12 @@
 
     def first_steps(self):
         p = self.p
-        n = p.n_row
-        order = (lambda: p.z, lambda: p.z + 1 - 2 * (p.z % 2), lambda: n - 1 - p.z, lambda: (p.z + n // 2) % n)
-        for source in order:
-            self.lanes.arrived(self.at(1, source(), p.k), self.one, self.r[1] + source())
+        for source in (p.z, self.far, self.near, self.cross):
+            self.lanes.arrived(self.at(1, source, p.k), self.one, self.r[1] + source)
 
             def make(source=source):
-                ref = self.at(1, source(), p.k)
-                return (ref, ref, self.two, self.s[3] + source(), self.r[3] + source())
+                ref = self.at(1, source, p.k)
+                return (ref, ref, self.two, self.s[3] + source, self.r[3] + source)
 
             self.lanes.send(make)
         self.to_other_core(1)
@@ -233,7 +207,7 @@
             self.second_steps((3,))
         else:
             self.z_step(int(name))
-            if int(name) == self.p.n_row - 1:
+            if name == "3":
                 self.z_done()
 
     def end(self):
@@ -267,11 +241,13 @@
 CHUNK = 512
 ROWS = 256
 BATCH = (6, 6, 6, 6, 7)
+FIRST = {"q": "x", "o": "y", "u": "y", "v": "y", "d": "y", "e": "y"}
+DOWN, UP, OUT, JOINED = "xyx", "xyx", "y", "xyx"
 SCHEDULE = {
     "first": {4: "oz uz", 5: "o1 u1 vz"},
     "turn": {0: "o2 u2 v1 dz", 2: "o3 u3 v2 d1"},
     "project": {0: "of v3 d2", 3: "uf d3", 6: "vf ez"},
-    "attend": {0: "df os e1", 1: "e2", 2: "us e3", 3: "ot ut", 4: "ef", 5: "vs", 6: "vt", 8: "cot", 9: "ds", 11: "dt"},
+    "attend": {0: "df os e1", 1: "e2", 2: "us e3", 3: "ot ut", 4: "ef", 5: "vs", 6: "vt", 7: "c1", 8: "c2 c3", 9: "ds", 11: "dt"},
     "mix": {1: "es"},
     "rise": {0: "et"},
 }
@@ -279,11 +255,12 @@
 
 def forward_kernel(
     dims, seq_ref, len_ref, tok_ref, cot_ref, qkv_ref, out_ref, up_ref, down_ref, norm_ref,
-    xt_out, wqkv_out, qkv_out, ctx_out, lse_out, output_out, gm_out, dctx_out, gout_out, gup_out, gdown_out, nsum_out,
+    xt_out, wqkv_out, qkv_out, ctx_out, lse_out, output_out, gm_out, dctx_out, gout_out, gup_out, part_x_out, part_y_out, nsum_out,
     tsend, half_qkv, half_out, half_up, pair_qkv, pair_out, pair_up,
     xt_v, x_v, w_v, wide_v, ctx_v, lse_v, wout_v, wup_v, wdown_v, norm_v, gains_v, cot_v, act_v, mixed_v, gsum_v, hl_v,
     output_v, down_v, attn_v, dctx_v, turn_v, nsum_v,
-    tok_send, tok_recv, norm_send, norm_recv, cot_send, cot_recv, w_send, w_recv, half_send, half_recv, local_sem, out_send, out_recv,
+    tok_send, tok_recv, norm_send, norm_recv, cot_send, cot_recv, w_send, w_recv, half_send, half_recv, local_sem, out_send, out_recv, r_send, r_recv,
+    *pieces,
 ):
     n_dp, n_row, n_col = dims
     p = Place(n_dp, n_row, n_col)
@@ -323,7 +300,7 @@
     region_qkv = rows_region(w_v, n_row)
     join(0, qkv_ref, half_qkv, pair_qkv)
     own_w = keep(pair_qkv, region_qkv(p.x, p.z, 1, p.y, p.k))
-    g_qkv = Gather(p, lanes, region_qkv, "x")
+    g_qkv = Gather(p, lanes, region_qkv, FIRST["q"])
     g_qkv.local = own_w
     g_qkv.start(pair_qkv)
     g_qkv.z_start()
@@ -370,14 +347,14 @@
         waves.append(gather)
 
     join(1, out_ref, half_out, pair_out)
-    wave(pair_out, rows_region(wout_v, n_row), "y")
+    wave(pair_out, rows_region(wout_v, n_row), FIRST["o"])
     join(2, up_ref, half_up, pair_up)
     cut = pair_up.shape[1] // 2
-    wave(pair_up.at[:, pl.ds(0, cut)], rows_region(wup_v, n_row, 0, cut), "y")
-    wave(pair_up.at[:, pl.ds(cut, cut)], rows_region(wup_v, n_row, cut, 2 * cut), "y")
+    wave(pair_up.at[:, pl.ds(0, cut)], rows_region(wup_v, n_row, 0, cut), FIRST["u"])
+    wave(pair_up.at[:, pl.ds(cut, cut)], rows_region(wup_v, n_row, cut, 2 * cut), FIRST["v"])
     cut = down_ref.shape[0] // 2
-    wave(down_ref.at[pl.ds(0, cut), :], lanes_region(wdown_v, n_dp, n_row, 0, cut), "y")
-    wave(down_ref.at[pl.ds(cut, cut), :], lanes_region(wdown_v, n_dp, n_row, cut, 2 * cut), "y")
+    wave(down_ref.at[pl.ds(0, cut), :], lanes_region(wdown_v, n_dp, n_row, 0, cut), FIRST["d"])
+    wave(down_ref.at[pl.ds(cut, cut), :], lanes_region(wdown_v, n_dp, n_row, cut, 2 * cut), FIRST["e"])
     lax.fori_loop(1, p.n, norm_start, 0)
     own_norm = keep(norm_ref, norm_v.at[p.flat])
 
@@ -392,14 +369,13 @@
     own_cot = keep(cot_ref.at[p.c], cot_v.at[p.c])
     names = dict(zip("ouvde", waves))
 
-    def begin_cot():
-        for i in range(1, n_col):
-            cot_copy(i).start()
+    def begin_cot(i):
+        cot_copy(i).start()
 
     def agenda(phase):
         table = {}
         for turn, steps in SCHEDULE.get(phase, {}).items():
-            table[turn] = [begin_cot if step == "cot" else functools.partial(names[step[0]].stage, step[1:]) for step in steps.split()]
+            table[turn] = [functools.partial(begin_cot, int(step[1:])) if step[0] == "c" else functools.partial(names[step[0]].stage, step[1:]) for step in steps.split()]
         return table
 
     first = agenda("first")
@@ -580,23 +556,34 @@
     keep(output_v.at[pl.ds(aligned(p.c * span, 16), span), :], output_out.at[p.c])
 
     def rise_back(step, carry):
-        at = pl.ds(aligned(step * 256, 256), 256)
-        back = product(down_v[...], wdown_v[:, :, :, at].reshape(width, 256))
+        at = pl.ds(aligned(step * 512, 512), 512)
+        back = product(down_v[...], wdown_v[:, :, :, at].reshape(width, 512))
         wide_v[:, at] = (back * wide_v[:, at].astype(F32)).astype(BF)
         return carry
 
-    lax.fori_loop(0, 4 * width // 256, rise_back, 0)
+    lax.fori_loop(0, 4 * width // 512, rise_back, 0)
     lanes.finish()
 
     def grad_down(step, carry):
-        at = pl.ds(aligned(step * 256, 256), 256)
-        wdown_v[:, :, :, at] = product(turn_v[...], act_v[:, at]).astype(BF).reshape(wdown_v.shape[:3] + (256,))
-        return carry
-
-    lax.fori_loop(0, 4 * width // 256, grad_down, 0)
-    keep(wdown_v, gdown_out)
+        at = pl.ds(aligned(step * 512, 512), 512)
+        wdown_v[:, :, :, at] = product(turn_v[...], act_v[:, at]).astype(BF).reshape(wdown_v.shape[:3] + (512,))
+        return carry
+
+    lax.fori_loop(0, 4 * width // 512, grad_down, 0)
+
+    rlanes = Lanes(r_send, r_recv)
+    early = []
+    piece_rows = wdown_v.shape[2] // len(DOWN)
+    for i, axis in enumerate(DOWN):
+        at = pl.ds(i * piece_rows, piece_rows)
+        piece = Reduce(
+            p, rlanes, wdown_v.at[:, 1 - p.k, at], wdown_v.at[:, p.k, at], pieces[2 * i:2 * i + 2] + (None, None, None), "lanes", axis
+        )
+        piece.start()
+        early.append(piece)
 
     def mix_back(step, carry):
+        run_events(step, {1: (early[0].one, early[1].one), 2: (early[2].one,)})
         at = pl.ds(aligned(step * ROWS, ROWS), ROWS)
         grad = gsum_v[at, :] + product_nt(wide_v[at, :], whole(wup_v))
         unit, scale = normal(mixed_v[at, :])
@@ -616,11 +603,11 @@
     keep(nsum_v, nsum_out)
 
     def grad_up(step, carry):
-        at = pl.ds(aligned(step * 256, 256), 256)
-        wup_v[:, :, :, at] = product(turn_v[...], wide_v[:, at]).astype(BF).reshape(wup_v.shape[:3] + (256,))
-        return carry
-
-    lax.fori_loop(0, 4 * width // 256, grad_up, 0)
+        at = pl.ds(aligned(step * 512, 512), 512)
+        wup_v[:, :, :, at] = product(turn_v[...], wide_v[:, at]).astype(BF).reshape(wup_v.shape[:3] + (512,))
+        return carry
+
+    lax.fori_loop(0, 4 * width // 512, grad_up, 0)
     keep(wup_v, gup_out)
 
     def grad_out(step, carry):
@@ -630,6 +617,10 @@
 
     lax.fori_loop(0, width // 256, grad_out, 0)
     keep(wout_v, gout_out)
+    outs = {"x": [part_x_out.at[i] for i in range(DOWN.count("x"))], "y": [part_y_out.at[i] for i in range(DOWN.count("y"))]}
+    for piece, axis in zip(early, DOWN):
+        piece.add_half(1)
+        keep(piece.b[1], outs[axis].pop(0))
 
     def small_wait(i, carry):
         norm_copy(i).wait_send()
@@ -651,6 +642,7 @@
         if not any(made is w for w in waited):
             made.wait()
     halves.finish()
+    rlanes.finish()
 
 
 def run_events(step, events):
@@ -687,10 +679,14 @@
         shape((rows, width), BF),
         shape(out_all, BF),
         shape(up_all, BF),
-        shape(down_all, BF),
+        shape((DOWN.count("x"), 2, dr // len(DOWN), dc * groups // 2), BF),
+        shape((DOWN.count("y"), dr // len(DOWN), dc * groups), BF),
         shape((8, width), F32),
     )
     vm = pltpu.VMEM
+    early_buffers = [
+        vm(size, BF) for axis in DOWN for size in piece_buffers("lanes", axis, 0, dr // len(DOWN), dc * groups, n_row, groups)[:2]
+    ]
     return pl.pallas_call(
         functools.partial(forward_kernel, dims),
         out_shape=outs,
@@ -716,7 +712,8 @@
             vm((width, rows), BF),
             vm((8, width), F32),
             DMA((n,)), DMA((n,)), DMA((n,)), DMA((n,)), DMA((n_col,)), DMA((n_col,)),
-            DMA((6 * 6 * n_row,)), DMA((6 * 5 * n_row,)), DMA((3,)), DMA((3,)), DMA((24,)), DMA((n_col,)), DMA((n_col,)),
+            DMA((6 * 5 * n_row,)), DMA((6 * 5 * n_row,)), DMA((3,)), DMA((3,)), DMA((24,)), DMA((n_col,)), DMA((n_col,)),
+            DMA((24,)), DMA((24,)), *early_buffers,
         ],
         compiler_params=pltpu.CompilerParams(
             collective_id=0, has_side_effects=True, vmem_limit_bytes=63 * 2**20
@@ -726,6 +723,12 @@
 
 
 BACK_CHUNK = 256
+SUMS = {
+    0: "u20 o00", 1: "u01 u11", 3: "u21 d13", 4: "d03", 6: "d23 d14", 7: "d04", 8: "a0 u02", 9: "o01 d24 d15", 10: "a1 d05",
+    12: "u12 d25", 14: "u22 u03", 16: "b0", 17: "u13 u04", 18: "o02 b1", 20: "u14 u05", 21: "a2 u23", 22: "u15", 23: "o03",
+}
+PACE = "0-16 | c1 a3 b2 u24 o04 | 16-32 | c2 a4 b3 c3 b4 c4"
+LATE = "o05 u25"
 
 
 def add_into(target, term):
@@ -745,8 +748,12 @@
     def __init__(self, place, lanes, theirs, mine, buffers, kind, first):
         self.p, self.lanes, self.theirs, self.mine, self.b = place, lanes, theirs, mine, buffers
         self.kind, self.axes = kind, ("x", "y") if first == "x" else ("y", "x")
-        self.s = [lanes.take(0, 1) for _ in range(3)] + [lanes.take(0, place.n_row - 1)]
-        self.r = [lanes.take(1, 1) for _ in range(3)] + [lanes.take(1, place.n_row - 1)]
+        self.s = [lanes.take(0, 1) for _ in range(3)] + [lanes.take(0, 3)]
+        self.r = [lanes.take(1, 1) for _ in range(3)] + [lanes.take(1, 3)]
+        n = place.n_row
+        self.far = (place.z + n // 2) % n
+        self.near = place.z + 1 - 2 * (place.z % 2)
+        self.cross = (self.near + n // 2) % n
 
     def start(self):
         p = self.p
@@ -798,42 +805,45 @@
     def three(self):
         p = self.p
         self.add_half(2)
-        for i in range(1, p.n_row):
-            def make(i=i):
-                target = (p.z + i) % p.n_row
-                return (self.part(target), self.b[3].at[i - 1], p.dev(z=target), self.s[3] + i - 1, self.r[3] + i - 1)
+        for i, target in enumerate((self.cross, self.near)):
+            def make(i=i, target=target):
+                return (self.part(target), self.b[3].at[1 - i], p.dev(z=self.near), self.s[3] + i, self.r[3] + i)
             self.lanes.send(make)
 
     def four(self):
         p = self.p
-        total = self.part(p.z)[...].astype(F32)
-        for i in range(1, p.n_row):
-            source = (p.z + p.n_row - i) % p.n_row
-            self.lanes.arrived(self.b[3].at[i - 1], p.dev(z=source), self.r[3] + i - 1)
-            total = total + self.b[3][i - 1].astype(F32)
-        return total
+        self.lanes.arrived(self.b[3].at[1], p.dev(z=self.near), self.r[3])
+        add_into(self.b[3].at[1], self.part(self.far))
+        self.lanes.send(lambda: (self.b[3].at[1], self.b[4], p.dev(z=self.far), self.s[3] + 2, self.r[3] + 2))
+
+    def five(self):
+        p = self.p
+        self.lanes.arrived(self.b[3].at[0], p.dev(z=self.near), self.r[3] + 1)
+        total = self.part(p.z)[...].astype(F32) + self.b[3][0].astype(F32)
+        self.lanes.arrived(self.b[4], p.dev(z=self.far), self.r[3] + 2)
+        return total + self.b[4][...].astype(F32)
 
 
 def piece_buffers(kind, first, lead, rows, columns, n_row, groups):
     if kind == "lanes":
         one = (2, rows, columns // 2) if first == "x" else (rows, columns)
-        return [(2, rows, columns), one, (rows, columns // 2), (n_row - 1, rows, columns // groups)]
+        return [(2, rows, columns), one, (rows, columns // 2), (2, rows, columns // groups), (rows, columns // groups)]
     one = (lead // 2, rows, columns) if first == "x" else (lead, rows, columns // 2)
-    return [(lead, rows, columns), one, (lead // 2, rows, columns // 2), (n_row - 1, rows, columns // 2)]
+    return [(lead, rows, columns), one, (lead // 2, rows, columns // 2), (2, rows, columns // 2), (rows, columns // 2)]
 
 
 def backward_kernel(
-    dims, plan, seq_ref, qkv_ref, ctx_ref, lse_ref, dctx_ref, xt_ref, w_ref, gm_ref, gout_ref, gup_ref, gdown_ref,
+    dims, plan, seq_ref, qkv_ref, ctx_ref, lse_ref, dctx_ref, xt_ref, w_ref, gm_ref, gout_ref, gup_ref, part_x_ref, part_y_ref,
     ngrad_ref, tgrad_ref, rqkv_ref, rout_ref, rup_ref, rdown_ref, nsum_ref, *scratch,
 ):
     n_dp, n_row, n_col = dims
     p = Place(n_dp, n_row, n_col)
     groups = n_dp * n_row
     (
-        qkv_v, ctx_v, lse_v, dctx_v, xt_v, w_v, gm_v, m_out, m_up, m_down, grad_v, dqt_v, dk_v, dv_v, acc_k, acc_v, dxt_v, trecv,
+        qkv_v, ctx_v, lse_v, dctx_v, xt_v, w_v, gm_v, m_out, m_up, ga_v, gb_v, gc_v, dqt_v, dk_v, dv_v, acc_k, acc_v, dxt_v, trecv,
         nrecv, fq, fo, fu, tok_send, tok_recv, norm_send, norm_recv, w_send, w_recv, local_sem,
-    ) = scratch[:29]
-    pieces = scratch[29:]
+    ) = scratch[:30]
+    pieces = scratch[30:]
     micro, slots, _, span = tgrad_ref.shape
     width, rows = ctx_ref.shape
     p.greet()
@@ -846,22 +856,31 @@
         return made
 
     needed = [keep(qkv_ref, qkv_v), keep(dctx_ref, dctx_v), keep(ctx_ref, ctx_v), keep(lse_ref, lse_v)]
-    mine_down = keep(gdown_ref.at[:, p.k], m_down)
     mine_up = keep(gup_ref.at[:, p.k], m_up)
     mine_out = keep(gout_ref.at[:, p.k], m_out)
-    later = [keep(w_ref, w_v), keep(gm_ref, gm_v), keep(xt_ref, xt_v)]
+    xt_load = keep(xt_ref, xt_v)
+    later = [keep(w_ref, w_v), keep(gm_ref, gm_v)]
     p.met()
     lanes = Lanes(w_send, w_recv)
     partner = p.dev(k=1 - p.k)
-    waves = {"down": [], "up": [], "out": [], "qkv": []}
-    whole = {"down": gdown_ref, "up": gup_ref, "out": gout_ref, "qkv": grad_v}
-    carried = {"down": m_down, "up": m_up, "out": m_out}
+    waves = {"down": [], "up": [], "out": [], "a": [], "b": [], "c": []}
+    parts = []
+    made_here = {"a": ga_v, "b": gb_v, "c": gc_v}
+    whole = {"up": gup_ref, "out": gout_ref, **made_here}
+    carried = {"up": m_up, "out": m_out}
+    sources = {"x": [part_x_ref.at[i] for i in range(DOWN.count("x"))], "y": [part_y_ref.at[i] for i in range(DOWN.count("y"))]}
     for index, (name, kind, first, low, count) in enumerate(plan):
+        if name == "down":
+            piece = Reduce(p, lanes, None, None, pieces[5 * index:5 * index + 5], kind, first)
+            parts.append(keep(sources[first].pop(0), piece.b[1]))
+            waves["down"].append(piece)
+            continue
         at = pl.ds(low, count)
         theirs = whole[name].at[:, 1 - p.k, at]
-        mine = carried[name].at[:, at] if name != "qkv" else grad_v.at[:, p.k, at]
-        waves[name].append(Reduce(p, lanes, theirs, mine, pieces[4 * index:4 * index + 4], kind, first))
-    d, u, o, q = waves["down"], waves["up"], waves["out"], waves["qkv"]
+        mine = made_here[name].at[:, p.k, at] if name in made_here else carried[name].at[:, at]
+        waves[name].append(Reduce(p, lanes, theirs, mine, pieces[5 * index:5 * index + 5], kind, first))
+    d, u, o = waves["down"], waves["up"], waves["out"]
+    joined = [waves[name][0] for name in "abc"]
 
     def norm_copy(i):
         target = (p.flat + i) % p.n
@@ -875,18 +894,20 @@
         norm_copy(i).start()
         return carry
 
-    d[0].start()
     u[0].start()
+    u[1].start()
+    for made, piece in zip(parts, d):
+        made.wait()
+        piece.send_half(2)
     lax.fori_loop(1, p.n, norm_start, 0)
     nrecv[p.flat] = ngrad_ref[p.flat]
     for made in needed:
         made.wait()
-    mine_down.wait()
     mine_up.wait()
     mine_out.wait()
 
     def finish_rows(piece, temp, result, low):
-        total = piece.four()
+        total = piece()
         count, across = total.shape[0], total.shape[1] // 2
         half_rows = result.shape[0] // 2
         temp[pl.ds(low, count), :] = jnp.where(p.k == 0, total[:, across:], total[:, :across])
@@ -899,37 +920,53 @@
     ends = []
 
     def finish_down(piece, low):
-        total = piece.four()
+        total = piece.five()
         rdown_ref[pl.ds(low, total.shape[0]), :] = total
 
     lows = {name: [low for other, _, _, low, _ in plan if other == name] for name in waves}
     down_end = [functools.partial(finish_down, piece, low) for piece, low in zip(d, lows["down"])]
-    up_end = [functools.partial(finish_rows, piece, fu, rup_ref, low) for piece, low in zip(u, lows["up"])]
-    out_end = [functools.partial(finish_rows, piece, fo, rout_ref, low) for piece, low in zip(o, lows["out"])]
-    qkv_end = [functools.partial(finish_rows, piece, fq, rqkv_ref, low) for piece, low in zip(q, lows["qkv"])]
-    events = {
-        0: (d[1].start, u[1].start),
-        1: (d[0].one, u[0].one),
-        2: (d[2].start, u[2].start, o[0].start),
-        4: (d[1].one,),
-        5: (u[1].one,),
-        6: (d[0].two,),
-        7: (u[0].two,),
-        9: (d[2].one,),
-        10: (u[2].one,),
-        11: (d[1].two,),
-        12: (u[1].two, d[0].three),
-        13: (u[0].three, o[0].one),
-        15: (d[2].two,),
-        16: (u[2].two, d[1].three),
-        17: (u[1].three,),
-        18: (o[0].two, down_end[0]),
-        19: (up_end[0],),
-        20: (d[2].three,),
-        21: (u[2].three, o[0].three),
-        22: (down_end[1],),
-        23: (up_end[1],),
+    up_end = [functools.partial(finish_rows, piece.five, fu, rup_ref, low) for piece, low in zip(u, lows["up"])]
+    out_end = [functools.partial(finish_rows, piece.five, fo, rout_ref, low) for piece, low in zip(o, lows["out"])]
+
+    def joined_total():
+        blocks = [[total[:, i * 128:(i + 1) * 128] for i in range(3)] for total in (piece.five() for piece in joined)]
+        middle = [piece[1] for piece in blocks]
+        queries = [piece[0] for piece in blocks] + middle + [piece[2] for piece in blocks]
+        return jnp.concatenate(queries, axis=1)
+
+    def joined_end():
+        finish_rows(joined_total, fq, rqkv_ref, 0)
+
+    xt = lambda: xt_v[...].reshape(width, rows)
+    pairs = width // 128
+
+    def grad_part(grad, number):
+        near, far = number, number + pairs // 2
+        columns = lambda pair: slice(pair * 128, pair * 128 + 128)
+        terms = (
+            lambda: product_nt(xt(), dqt_v[columns(near), :]), lambda: product_nt(xt(), dqt_v[columns(far), :]),
+            lambda: product(xt(), dk_v[:, columns(near)]), lambda: product(xt(), dk_v[:, columns(far)]),
+            lambda: product(xt(), dv_v[:, columns(near)]), lambda: product(xt(), dv_v[:, columns(far)]),
+        )
+        for i, term in enumerate(terms):
+            grad[:, :, :, columns(i)] = term().astype(BF).reshape(groups, 2, -1, 128)
+        joined[number].start()
+
+    def first_part():
+        xt_load.wait()
+        grad_part(ga_v, 0)
+
+    table = {
+        letter + str(i) + str(stage): act
+        for letter, group, ends_ in (("d", d, down_end), ("u", u, up_end), ("o", o, out_end))
+        for i, (piece, end) in enumerate(zip(group, ends_))
+        for stage, act in enumerate((piece.start, piece.one, piece.two, piece.three, piece.four, end))
     }
+    for letter, piece in zip("abc", joined):
+        for stage, act in enumerate((piece.one, piece.two, piece.three, piece.four)):
+            table[letter + str(stage + 1)] = act
+    table.update({"a0": first_part, "b0": functools.partial(grad_part, gb_v, 1), "c0": functools.partial(grad_part, gc_v, 2)})
+    events = {turn: [table[step] for step in steps.split()] for turn, steps in SUMS.items()}
     length_bias = jnp.where(lax.broadcasted_iota(jnp.int32, (rows, 1), 0) < seq_ref[1, p.c, seq_ref[0, p.c, p.g]], 0.0, NEGATIVE)
     chunks = rows // BACK_CHUNK
 
@@ -939,7 +976,8 @@
                 for a in acts:
                     a()
             pl.when(step == when_)(act)
-        pair, at_row = step // chunks, step % chunks
+        turn, at_row = step // chunks, step % chunks
+        pair = turn % 2 * (pairs // 2) + turn // 2
         columns = [pl.ds(aligned(i * width + pair * 128, 128), 128) for i in range(3)]
         keys, values = qkv_v[:, columns[1]], qkv_v[:, columns[2]]
         keys_t = keys.T
@@ -997,7 +1035,19 @@
 
     half_groups = groups // 2
     half_width = width // 2
-    for part in range(2):
+
+    def tok_batch(part, low, high):
+        def one(i, carry):
+            target = part * half_groups * n_col + (p.flat + i * 5) % (half_groups * n_col)
+
+            @pl.when(target != p.flat)
+            def _():
+                tok_copy(target).start()
+            return carry
+
+        lax.fori_loop(low, high, one, 0)
+
+    def grad_input(part):
         near = pl.ds(part * half_groups, half_groups)
         w_rows = lambda i: w_v[near, :, :, i * width:(i + 1) * width].reshape(half_width, width)
         total = gm_v[:, part * half_width:(part + 1) * half_width].T
@@ -1006,44 +1056,25 @@
         total = total + product_nt(w_rows(2), dv_v[...])
         dxt_v[near] = total.astype(BF).reshape(half_groups, width // groups, rows)
 
-        def tok_start(i, carry, part=part):
-            base = part * half_groups * n_col
-            target = base + (p.flat + i) % (half_groups * n_col)
-
-            @pl.when(target != p.flat)
-            def _():
-                tok_copy(target).start()
-            return carry
-
-        lax.fori_loop(0, half_groups * n_col, tok_start, 0)
-    own_tok = keep(dxt_v.at[p.g, :, pl.ds(aligned(p.c * span, 128), span)], trecv.at[p.c * slots + p.g])
-
-    def grad_q(i, carry):
-        at = pl.ds(aligned(i * 256, 256), 256)
-        grad_v[:, :, :, at] = product_nt(xt_v[...].reshape(width, rows), dqt_v[at, :]).astype(BF).reshape(groups, 2, -1, 256)
-        return carry
-
-    def grad_k(i, carry):
-        at = pl.ds(aligned(i * 256, 256), 256)
-        to = lambda j: pl.ds(aligned(j * width + i * 256, 256), 256)
-        xt = xt_v[...].reshape(width, rows)
-        grad_v[:, :, :, to(1)] = product(xt, dk_v[:, at]).astype(BF).reshape(groups, 2, -1, 256)
-        grad_v[:, :, :, to(2)] = product(xt, dv_v[:, at]).astype(BF).reshape(groups, 2, -1, 256)
-        return carry
-
-    lax.fori_loop(0, width // 256, grad_q, 0)
-    lax.fori_loop(0, width // 256, grad_k, 0)
-    for piece in q:
-        piece.start()
-    for piece in q:
-        piece.one()
-    down_end[2]()
-    up_end[2]()
-    out_end[0]()
-    for piece in q:
-        piece.two()
-    for piece in q:
-        piece.three()
+    count = half_groups * n_col
+    table["c0"]()
+    grad_input(0)
+    made_parts = 1
+    for step in PACE.replace("|", " ").split():
+        if "-" not in step:
+            table[step]()
+            continue
+        low, high = (int(number) for number in step.split("-"))
+        if high > count and made_parts == 1:
+            grad_input(1)
+            made_parts = 2
+            own_tok = keep(dxt_v.at[p.g, :, pl.ds(aligned(p.c * span, 128), span)], trecv.at[p.c * slots + p.g])
+        for part in range(2):
+            first, last = max(low, part * count) - part * count, min(high, part * count + count) - part * count
+            if first < last:
+                tok_batch(part, first, last)
+    for step in LATE.split():
+        table[step]()
 
     def norm_wait(i, carry):
         source = (p.flat + p.n - i) % p.n
@@ -1056,8 +1087,7 @@
 
     lax.fori_loop(1, p.n, norm_wait, 0)
     nsum_ref[...] = jnp.sum(nrecv[...], axis=0)
-    for end in qkv_end:
-        end()
+    joined_end()
     own_tok.wait()
 
     def tok_wait(i, carry):
@@ -1082,7 +1112,7 @@
     lanes.finish()
 
 
-def backward(dims, seq_order, lengths, qkv, ctx_t, lse, d_context, xt, w_qkv, g_mixed, g_out, g_up, g_down_t, n_grads):
+def backward(dims, seq_order, lengths, qkv, ctx_t, lse, d_context, xt, w_qkv, g_mixed, g_out, g_up, part_x, part_y, n_grads):
     n_dp, n_row, n_col = dims
     groups, n = n_dp * n_row, n_dp * n_row * n_col
     micro, slots = seq_order.shape
@@ -1090,33 +1120,39 @@
     feats, span = width // groups, rows // n_col
     shape = jax.ShapeDtypeStruct
     plan, buffers = [], []
-    for name, grad, kind, first, count in (
-        ("down", g_down_t, "lanes", "x", 3), ("up", g_up, "rows", "y", 3), ("out", g_out, "rows", "x", 1),
-        ("qkv", w_qkv, "rows", "y", 3),
+    for name, grad, kind, axes in (
+        ("down", part_y, "lanes", DOWN), ("up", g_up, "rows", UP), ("out", g_out, "rows", OUT),
+        *((letter, g_out, "rows", axis) for letter, axis in zip("abc", JOINED)),
     ):
-        lead, _, across, columns = grad.shape
-        each = across // count
-        for i in range(count):
-            plan.append((name, kind, first, i * each, each))
-            buffers += [pltpu.VMEM(b, BF) for b in piece_buffers(kind, first, lead, each, columns, n_row, groups)]
+        if name == "down":
+            lead, each, columns = 2, part_y.shape[1], part_y.shape[2]
+        else:
+            lead, _, across, columns = grad.shape
+            each = across // len(axes)
+        for i, axis in enumerate(axes):
+            plan.append((name, kind, axis, i * each, each))
+            sizes = piece_buffers(kind, axis, lead, each, columns, n_row, groups)
+            if name == "down":
+                sizes[0] = (16, 128)
+            buffers += [pltpu.VMEM(size, BF) for size in sizes]
     outs = (
         shape((micro, slots, feats, span), BF),
         shape((w_qkv.shape[2] * 2, w_qkv.shape[3] // n_col), F32),
         shape((g_out.shape[2] * 2, g_out.shape[3] // n_col), F32),
         shape((g_up.shape[2] * 2, g_up.shape[3] // n_col), F32),
-        shape((g_down_t.shape[2], g_down_t.shape[3] // groups), F32),
+        shape((len(DOWN) * part_y.shape[1], part_y.shape[2] // groups), F32),
         shape(n_grads.shape[1:], F32),
     )
     vm = lambda like, kind=BF: pltpu.VMEM(like.shape, kind)
     temps = [pltpu.VMEM((g.shape[2], g.shape[3] // n_col), F32) for g in (w_qkv, g_out, g_up)]
-    carried = [pltpu.VMEM((g.shape[0],) + g.shape[2:], BF) for g in (g_out, g_up, g_down_t)]
+    carried = [pltpu.VMEM((g.shape[0],) + g.shape[2:], BF) for g in (g_out, g_up)]
     return pl.pallas_call(
         functools.partial(backward_kernel, dims, plan),
         out_shape=outs,
-        in_specs=[SM, ANY, ANY, ANY, ANY, ANY, ANY, ANY, ANY, ANY, ANY, VM],
+        in_specs=[SM, ANY, ANY, ANY, ANY, ANY, ANY, ANY, ANY, ANY, ANY, ANY, VM],
         out_specs=[VM, VM, VM, VM, VM, VM],
         scratch_shapes=[
-            vm(qkv), vm(ctx_t), vm(lse, F32), vm(d_context), vm(xt), vm(w_qkv), vm(g_mixed, F32), *carried, vm(w_qkv),
+            vm(qkv), vm(ctx_t), vm(lse, F32), vm(d_context), vm(xt), vm(w_qkv), vm(g_mixed, F32), *carried, vm(g_out), vm(g_out), vm(g_out),
             pltpu.VMEM((width, rows), BF), pltpu.VMEM((rows, width), BF), pltpu.VMEM((rows, width), BF),
             pltpu.VMEM((rows, 128), F32), pltpu.VMEM((rows, 128), F32),
             pltpu.VMEM((groups, feats, rows), BF), pltpu.VMEM((micro * slots, feats, span), BF),
@@ -1128,7 +1164,7 @@
             collective_id=1, has_side_effects=True, vmem_limit_bytes=62 * 2**20
         ),
         name="backward_part",
-    )(jnp.stack([seq_order, lengths]), qkv, ctx_t, lse, d_context, xt, w_qkv, g_mixed, g_out, g_up, g_down_t, n_grads)
+    )(jnp.stack([seq_order, lengths]), qkv, ctx_t, lse, d_context, xt, w_qkv, g_mixed, g_out, g_up, part_x, part_y, n_grads)
 def layer_norm(values, factor, offset):
     average = jnp.mean(values, axis=-1, keepdims=True)
     centered = values - average
@@ -1232,7 +1268,7 @@
     micro, slots, span, feats = tokens.shape
     width = cotangent.shape[3]
     rows = span * n_col
-    direct = n_dp == 2 and n_col == 4 and feats % 32 == 0 and w_qkv.shape[0] % 32 == 0
+    direct = n_dp == 2 and n_row == 4 and n_col == 4 and feats % 32 == 0 and w_qkv.shape[0] % 32 == 0
     tok_t = jnp.swapaxes(tokens, 2, 3)
     w_down_t = w_down.T
     norms = jnp.stack([gain_one, shift_one, gain_two, shift_two])
@@ -1245,7 +1281,7 @@
         here = lane[None, :] == (place * each) % 128 + jnp.arange(each, dtype=jnp.int32)[:, None]
         packed = jnp.sum(jnp.where(here[None], norms[:, :, None].astype(F32), 0.0), axis=1).astype(BF)
         packed = jnp.pad(packed, ((0, 12), (0, 0)))
-        xt, w_joined, qkv, context_t, lse, output, g_mixed, d_context, g_out, g_up, g_down_t, norm_grads = forward(
+        xt, w_joined, qkv, context_t, lse, output, g_mixed, d_context, g_out, g_up, part_x, part_y, norm_grads = forward(
             dims, seq_order, lengths, tok_t, cotangent[:, 0], w_qkv, w_out, w_up, w_down_t, packed
         )
         norm_grads = norm_grads[:4]
@@ -1269,7 +1305,7 @@
         n_grads = jnp.pad(n_grads, ((0, 0), (0, 4), (0, 128 - each)))
         tgrad, r_qkv, r_out, r_up, r_down_t, n_sum = backward(
             dims, seq_order, lengths, qkv, context_t, lse, d_context, xt, w_joined, g_mixed,
-            g_out, g_up, g_down_t, n_grads,
+            g_out, g_up, part_x, part_y, n_grads,
         )
         n_sum = n_sum[:4, :each]
     else:

time: 304 us -> 299 us (0.984)
  Pallas kernels: 290 us -> 286 us
    pallas_call x1, Pallas kernels: 121 us -> 117 us  [backward(): pl.pallas_call(functools.partial(backward_kernel, dims, plan), out_shape=...]
where the time goes in v1:
time: 299 us; the launch traced here: 298 us
  Pallas kernels  286 us (96%)
  local copies, waits for them, and re-layouts  9.41 us (3%)
    pallas_call x1, Pallas kernels, forward(): pl.pallas_call(functools.partial(forward_kernel, dims), out_shape=outs, i...  169 us
    pallas_call x1, Pallas kernels, backward(): pl.pallas_call(functools.partial(backward_kernel, dims, plan), out_shape=...  117 us

profile of v1, /device:TPU:0, one launch (start us, length us, event | category | flops | bytes accessed | tf_op | source)
XLA Modules:
  0.0 298.2 jit_solution(12780432782982814914)
XLA Ops:
  0.7 0.7 maximum_convert_fusion
  1.4 1.3 pad_add_fusion.seq_ref
  2.7 0.1 iota_compare_fusion
  2.8 0.1 select_reduce_fusion
  2.9 0.6 pad.8.norm_ref
  3.5 168.6 %forward_part.1 = (bf16[8,96,1024]{2,1,0:T(8,128)(2,1)}, bf16[8,2,48,2304]{3,2,1,0:T(8,128)(2,1)}, bf16[1024,2304]{1,0:T(8,128)(2,1)}, bf16[768,1024]{1,0:T(8,12...) custom-call(s32[4,8]{1,0:T(4,128)} %seq_ref.1, ...), custom_call_target="tpu_custom_call" | custom-call | tf_op jit(solution)/shard_map/forward_part/pallas_call | solution.py:690
  172.1 0.7 slice.20
  172.8 0.1 reshape.81
  173.0 0.7 pad.9.ngrad_ref
  173.7 0.0 copy-start
  173.7 117.2 %backward_part.1 = (bf16[4,8,96,256]{3,2,1,0:T(8,128)(2,1)}, f32[96,576]{1,0:T(8,128)}, f32[96,192]{1,0:T(8,128)}, f32[96,768]{1,0:T(8,128)}, f32[192,384]{1,0:T(8,128)}, /*index=5*/f32[8,128]{1,0:T(8,128)}) custom-call(s32[2,4,8]{2,1,0:T(4,128)} %pad_add_fusion.seq_ref, bf16[1024,2304]{1,0:T(8,128)(2,1)} %get-tuple-element.30.qkv_ref, ...), custom_call_target="tpu_custom_call" | custom-call | tf_op jit(solution)/shard_map/backward_part/pallas_call | solution.py:1149
  290.9 1.4 slice_bitcast_fusion
  292.3 0.0 copy-done
  292.3 0.0 copy-start.1
  292.3 1.1 copy.35
  293.4 0.8 copy-done.1
  294.2 0.0 copy-start.4
  294.2 0.0 copy-start.5
  294.2 0.0 copy-start.3
  294.2 0.0 copy-start.2
  294.2 1.1 copy.36
  295.4 0.0 copy-done.4
  295.4 0.7 copy.37
  296.1 0.0 copy-done.5
  296.1 0.6 copy.38
  296.7 0.0 copy-done.3
  296.7 0.7 copy.39
  297.5 0.0 copy-done.2
  297.5 0.7 copy.40
  (2 shorter events, 0.0 us)
Async XLA Ops:
  173.7 118.6 %copy-start = (bf16[4,256,768]{2,1,0:T(8,128)(2,1)S(1)}, bf16[4,256,768]{2,1,0:T(8,128)(2,1)}, u32[]{:S(2)}) copy-start(bf16[4,256,768]{2,1,0:T(8,128)(2,1)} %get-tuple-element.29) | copy-start | bytes 4718596
  292.3 2.0 copy-start.1
  294.2 1.2 copy-start.4
  294.2 1.9 copy-start.5
  294.2 2.5 copy-start.3
  294.2 3.2 %copy-start.2 = (f32[192,384]{1,0:T(8,128)S(1)}, f32[192,384]{1,0:T(8,128)}, u32[]{:S(2)}) copy-start(f32[192,384]{1,0:T(8,128)} %get-tuple-element.46) | copy-start | bytes 884740

commit v2 on v1

--- a/solution.py
+++ b/solution.py
@@ -244,12 +244,12 @@
 FIRST = {"q": "x", "o": "y", "u": "y", "v": "y", "d": "y", "e": "y"}
 DOWN, UP, OUT, JOINED = "xyx", "xyx", "y", "xyx"
 SCHEDULE = {
-    "first": {4: "oz uz", 5: "o1 u1 vz"},
-    "turn": {0: "o2 u2 v1 dz", 2: "o3 u3 v2 d1"},
-    "project": {0: "of v3 d2", 3: "uf d3", 6: "vf ez"},
-    "attend": {0: "df os e1", 1: "e2", 2: "us e3", 3: "ot ut", 4: "ef", 5: "vs", 6: "vt", 7: "c1", 8: "c2 c3", 9: "ds", 11: "dt"},
-    "mix": {1: "es"},
-    "rise": {0: "et"},
+    "first": {4: ("oz", "uz",), 5: ("o1", "u1", "vz",)},
+    "turn": {0: ("o2", "u2", "v1", "dz",), 2: ("o3", "u3", "v2", "d1",)},
+    "project": {0: ("of", "v3", "d2",), 3: ("uf", "d3",), 6: ("vf", "ez",)},
+    "attend": {0: ("df", "os", "e1",), 1: ("e2",), 2: ("us", "e3",), 3: ("ot", "ut",), 4: ("ef",), 5: ("vs",), 6: ("vt",), 7: ("c1",), 8: ("c2", "c3",), 9: ("ds",), 11: ("dt",)},
+    "mix": {1: ("es",)},
+    "rise": {0: ("et",)},
 }
 
 
@@ -375,7 +375,7 @@
     def agenda(phase):
         table = {}
         for turn, steps in SCHEDULE.get(phase, {}).items():
-            table[turn] = [functools.partial(begin_cot, int(step[1:])) if step[0] == "c" else functools.partial(names[step[0]].stage, step[1:]) for step in steps.split()]
+            table[turn] = [functools.partial(begin_cot, int(step[1:])) if step[0] == "c" else functools.partial(names[step[0]].stage, step[1:]) for step in steps]
         return table
 
     first = agenda("first")
@@ -539,8 +539,8 @@
         output_v[at, :] = (unit * gain_two + shift_two).astype(BF)
         per = span // ROWS
         cot = cot_v[step // per, pl.ds(aligned(step % per * ROWS, ROWS), ROWS), :].astype(F32)
-        nsum_v[2:3, :] += jnp.sum(cot * unit, axis=0, keepdims=True)
-        nsum_v[3:4, :] += jnp.sum(cot, axis=0, keepdims=True)
+        nsum_v[2:3, :width] += jnp.sum(cot * unit, axis=0, keepdims=True)
+        nsum_v[3:4, :width] += jnp.sum(cot, axis=0, keepdims=True)
         grad = normal_back(cot, unit, scale, gain_two)
         gsum_v[at, :] = grad
         down_v[at, :] = grad.astype(BF)
@@ -587,8 +587,8 @@
         at = pl.ds(aligned(step * ROWS, ROWS), ROWS)
         grad = gsum_v[at, :] + product_nt(wide_v[at, :], whole(wup_v))
         unit, scale = normal(mixed_v[at, :])
-        nsum_v[0:1, :] += jnp.sum(grad * unit, axis=0, keepdims=True)
-        nsum_v[1:2, :] += jnp.sum(grad, axis=0, keepdims=True)
+        nsum_v[0:1, :width] += jnp.sum(grad * unit, axis=0, keepdims=True)
+        nsum_v[1:2, :width] += jnp.sum(grad, axis=0, keepdims=True)
         grad = normal_back(grad, unit, scale, gain_one)
         gsum_v[at, :] = grad
         low = grad.astype(BF)
@@ -681,7 +681,7 @@
         shape(up_all, BF),
         shape((DOWN.count("x"), 2, dr // len(DOWN), dc * groups // 2), BF),
         shape((DOWN.count("y"), dr // len(DOWN), dc * groups), BF),
-        shape((8, width), F32),
+        shape((8, width + 256), F32),
     )
     vm = pltpu.VMEM
     early_buffers = [
@@ -710,7 +710,7 @@
             vm((rows, width), F32), vm((rows, width), F32),
             vm((rows, width), BF), vm((rows, width), BF), vm((rows, width), BF), vm((rows, width), BF), vm((rows, width), BF),
             vm((width, rows), BF),
-            vm((8, width), F32),
+            vm((8, width + 256), F32),
             DMA((n,)), DMA((n,)), DMA((n,)), DMA((n,)), DMA((n_col,)), DMA((n_col,)),
             DMA((6 * 5 * n_row,)), DMA((6 * 5 * n_row,)), DMA((3,)), DMA((3,)), DMA((24,)), DMA((n_col,)), DMA((n_col,)),
             DMA((24,)), DMA((24,)), *early_buffers,
@@ -724,11 +724,11 @@
 
 BACK_CHUNK = 256
 SUMS = {
-    0: "u20 o00", 1: "u01 u11", 3: "u21 d13", 4: "d03", 6: "d23 d14", 7: "d04", 8: "a0 u02", 9: "o01 d24 d15", 10: "a1 d05",
-    12: "u12 d25", 14: "u22 u03", 16: "b0", 17: "u13 u04", 18: "o02 b1", 20: "u14 u05", 21: "a2 u23", 22: "u15", 23: "o03",
+    0: ("u20", "o00",), 1: ("u01", "u11",), 3: ("u21", "d13",), 4: ("d03",), 6: ("d23", "d14",), 7: ("d04",), 8: ("a0", "u02",), 9: ("o01", "d24", "d15",), 10: ("a1", "d05",),
+    12: ("u12", "d25",), 14: ("u22", "u03",), 16: ("b0",), 17: ("u13", "u04",), 18: ("o02", "b1",), 20: ("u14", "u05",), 21: ("a2", "u23",), 22: ("u15",), 23: ("o03",),
 }
-PACE = "0-16 | c1 a3 b2 u24 o04 | 16-32 | c2 a4 b3 c3 b4 c4"
-LATE = "o05 u25"
+PACE = ((0, 16), "c1", "a3", "b2", "u24", "o04", (16, 32), "c2", "a4", "b3", "c3", "b4", "c4")
+LATE = ("o05", "u25")
 
 
 def add_into(target, term):
@@ -833,7 +833,7 @@
 
 
 def backward_kernel(
-    dims, plan, seq_ref, qkv_ref, ctx_ref, lse_ref, dctx_ref, xt_ref, w_ref, gm_ref, gout_ref, gup_ref, part_x_ref, part_y_ref,
+    dims, plan, seq_ref, len_ref, qkv_ref, ctx_ref, lse_ref, dctx_ref, xt_ref, w_ref, gm_ref, gout_ref, gup_ref, part_x_ref, part_y_ref,
     ngrad_ref, tgrad_ref, rqkv_ref, rout_ref, rup_ref, rdown_ref, nsum_ref, *scratch,
 ):
     n_dp, n_row, n_col = dims
@@ -882,10 +882,13 @@
     d, u, o = waves["down"], waves["up"], waves["out"]
     joined = [waves[name][0] for name in "abc"]
 
+    def window(device):
+        return pl.ds(aligned(device * (width // p.n) // 128 * 128, 128), 256)
+
     def norm_copy(i):
         target = (p.flat + i) % p.n
         return pltpu.make_async_remote_copy(
-            src_ref=ngrad_ref.at[target], dst_ref=nrecv.at[p.flat],
+            src_ref=ngrad_ref.at[:, window(target)], dst_ref=nrecv.at[p.flat],
             send_sem=norm_send.at[i], recv_sem=norm_recv.at[i],
             device_id=p.of_flat(target), device_id_type=MESH,
         )
@@ -900,7 +903,7 @@
         made.wait()
         piece.send_half(2)
     lax.fori_loop(1, p.n, norm_start, 0)
-    nrecv[p.flat] = ngrad_ref[p.flat]
+    nrecv[p.flat] = ngrad_ref[:, window(p.flat)]
     for made in needed:
         made.wait()
     mine_up.wait()
@@ -966,8 +969,8 @@
         for stage, act in enumerate((piece.one, piece.two, piece.three, piece.four)):
             table[letter + str(stage + 1)] = act
     table.update({"a0": first_part, "b0": functools.partial(grad_part, gb_v, 1), "c0": functools.partial(grad_part, gc_v, 2)})
-    events = {turn: [table[step] for step in steps.split()] for turn, steps in SUMS.items()}
-    length_bias = jnp.where(lax.broadcasted_iota(jnp.int32, (rows, 1), 0) < seq_ref[1, p.c, seq_ref[0, p.c, p.g]], 0.0, NEGATIVE)
+    events = {turn: [table[step] for step in steps] for turn, steps in SUMS.items()}
+    length_bias = jnp.where(lax.broadcasted_iota(jnp.int32, (rows, 1), 0) < len_ref[p.c, seq_ref[p.c, p.g]], 0.0, NEGATIVE)
     chunks = rows // BACK_CHUNK
 
     def attend(step, carry):
@@ -1060,11 +1063,11 @@
     table["c0"]()
     grad_input(0)
     made_parts = 1
-    for step in PACE.replace("|", " ").split():
-        if "-" not in step:
+    for step in PACE:
+        if isinstance(step, str):
             table[step]()
             continue
-        low, high = (int(number) for number in step.split("-"))
+        low, high = step
         if high > count and made_parts == 1:
             grad_input(1)
             made_parts = 2
@@ -1073,7 +1076,7 @@
             first, last = max(low, part * count) - part * count, min(high, part * count + count) - part * count
             if first < last:
                 tok_batch(part, first, last)
-    for step in LATE.split():
+    for step in LATE:
         table[step]()
 
     def norm_wait(i, carry):
@@ -1105,7 +1108,7 @@
         for s in range(slots):
             place = jnp.int32(0)
             for j in range(slots):
-                place = jnp.where(seq_ref[0, m, j] == s, jnp.int32(j), place)
+                place = jnp.where(seq_ref[m, j] == s, jnp.int32(j), place)
             tgrad_ref[m, s] = trecv[m * slots + place]
     for end in ends:
         end()
@@ -1141,7 +1144,7 @@
         shape((g_out.shape[2] * 2, g_out.shape[3] // n_col), F32),
         shape((g_up.shape[2] * 2, g_up.shape[3] // n_col), F32),
         shape((len(DOWN) * part_y.shape[1], part_y.shape[2] // groups), F32),
-        shape(n_grads.shape[1:], F32),
+        shape((8, 256), F32),
     )
     vm = lambda like, kind=BF: pltpu.VMEM(like.shape, kind)
     temps = [pltpu.VMEM((g.shape[2], g.shape[3] // n_col), F32) for g in (w_qkv, g_out, g_up)]
@@ -1149,14 +1152,14 @@
     return pl.pallas_call(
         functools.partial(backward_kernel, dims, plan),
         out_shape=outs,
-        in_specs=[SM, ANY, ANY, ANY, ANY, ANY, ANY, ANY, ANY, ANY, ANY, ANY, VM],
+        in_specs=[SM, SM, ANY, ANY, ANY, ANY, ANY, ANY, ANY, ANY, ANY, ANY, ANY, VM],
         out_specs=[VM, VM, VM, VM, VM, VM],
         scratch_shapes=[
             vm(qkv), vm(ctx_t), vm(lse, F32), vm(d_context), vm(xt), vm(w_qkv), vm(g_mixed, F32), *carried, vm(g_out), vm(g_out), vm(g_out),
             pltpu.VMEM((width, rows), BF), pltpu.VMEM((rows, width), BF), pltpu.VMEM((rows, width), BF),
             pltpu.VMEM((rows, 128), F32), pltpu.VMEM((rows, 128), F32),
             pltpu.VMEM((groups, feats, rows), BF), pltpu.VMEM((micro * slots, feats, span), BF),
-            vm(n_grads, F32), *temps,
+            pltpu.VMEM((n, 8, 256), F32), *temps,
             DMA((n,)), DMA((n,)), DMA((n,)), DMA((n,)),
             DMA((80,)), DMA((80,)), DMA((16,)), *buffers,
         ],
@@ -1164,7 +1167,7 @@
             collective_id=1, has_side_effects=True, vmem_limit_bytes=62 * 2**20
         ),
         name="backward_part",
-    )(jnp.stack([seq_order, lengths]), qkv, ctx_t, lse, d_context, xt, w_qkv, g_mixed, g_out, g_up, part_x, part_y, n_grads)
+    )(seq_order, lengths, qkv, ctx_t, lse, d_context, xt, w_qkv, g_mixed, g_out, g_up, part_x, part_y, n_grads)
 def layer_norm(values, factor, offset):
     average = jnp.mean(values, axis=-1, keepdims=True)
     centered = values - average
@@ -1284,7 +1287,6 @@
         xt, w_joined, qkv, context_t, lse, output, g_mixed, d_context, g_out, g_up, part_x, part_y, norm_grads = forward(
             dims, seq_order, lengths, tok_t, cotangent[:, 0], w_qkv, w_out, w_up, w_down_t, packed
         )
-        norm_grads = norm_grads[:4]
     else:
         offset = jnp.arange(micro, dtype=jnp.int32)[:, None] * slots
         sent = take_blocks(tok_t.reshape(micro * slots, feats, span), (seq_order + offset).reshape(-1))
@@ -1301,13 +1303,11 @@
         f_down_t = whole(w_down_t, "col", ("dp", "row"))
         f_norms = lax.all_gather(norms, everyone, axis=1, tiled=True)
     if direct:
-        n_grads = jnp.swapaxes(norm_grads.reshape(4, width // each, each), 0, 1)
-        n_grads = jnp.pad(n_grads, ((0, 0), (0, 4), (0, 128 - each)))
         tgrad, r_qkv, r_out, r_up, r_down_t, n_sum = backward(
             dims, seq_order, lengths, qkv, context_t, lse, d_context, xt, w_joined, g_mixed,
-            g_out, g_up, part_x, part_y, n_grads,
+            g_out, g_up, part_x, part_y, norm_grads,
         )
-        n_sum = n_sum[:4, :each]
+        n_sum = lax.dynamic_slice(n_sum, (0, place * each % 128), (4, each))
     else:
         gains = [f_norms[i].astype(F32) for i in range(4)]
         x = xt.T

time: 299 us -> 296 us (0.990)
  no operation moved by 1% of the time
where the time goes in v2:
time: 296 us
  Pallas kernels  287 us (97%)
  local copies, waits for them, and re-layouts  7.81 us (3%)
    pallas_call x1, Pallas kernels, forward(): pl.pallas_call(functools.partial(forward_kernel, dims), out_shape=outs, i...  169 us
    pallas_call x1, Pallas kernels, backward(): pl.pallas_call(functools.partial(backward_kernel, dims, plan), out_shape=...  118 us

profile of v2, /device:TPU:0, one launch (start us, length us, event | category | flops | bytes accessed | tf_op | source)
XLA Modules:
  0.0 296.1 jit_solution(18336207409580329967)
XLA Ops:
  0.7 0.7 maximum_convert_fusion
  1.4 0.1 iota_compare_fusion
  1.5 0.1 select_reduce_fusion
  1.6 0.6 pad.4.norm_ref
  2.2 168.6 %forward_part.1 = (bf16[8,96,1024]{2,1,0:T(8,128)(2,1)}, bf16[8,2,48,2304]{3,2,1,0:T(8,128)(2,1)}, bf16[1024,2304]{1,0:T(8,128)(2,1)}, bf16[768,1024]{1,0:T(8,12...) custom-call(s32[4,8]{1,0:T(4,128)} %seq_ref.3, ...), custom_call_target="tpu_custom_call" | custom-call | tf_op jit(solution)/shard_map/forward_part/pallas_call | solution.py:690
  170.8 0.0 copy-start
  170.8 118.1 %backward_part.1 = (bf16[4,8,96,256]{3,2,1,0:T(8,128)(2,1)}, f32[96,576]{1,0:T(8,128)}, f32[96,192]{1,0:T(8,128)}, f32[96,768]{1,0:T(8,128)}, f32[192,384]{1,0:T(8,128)}, /*index=5*/f32[8,256]{1,0:T(8,128)}) custom-call(s32[4,8]{1,0:T(4,128)} %seq_ref.3, s32[4,8]{1,0:T(4,128)} %len_ref.3, bf16[1024,2304]{1,0:T(8,128)(2,1)} %get-tuple-element.30.qkv_ref, ...), custom_call_target="tpu_custom_call" | custom-call | tf_op jit(solution)/shard_map/backward_part/pallas_call | solution.py:1152
  288.9 0.8 constant_dynamic-slice_fusion
  289.7 0.5 slice_bitcast_fusion
  290.2 0.0 copy-done
  290.2 0.0 copy-start.1
  290.2 1.1 copy.30
  291.4 0.8 copy-done.1
  292.2 0.0 copy-start.4
  292.2 0.0 copy-start.5
  292.2 0.0 copy-start.3
  292.2 0.0 copy-start.2
  292.2 1.1 copy.31
  293.4 0.0 copy-done.4
  293.4 0.7 copy.32
  294.1 0.0 copy-done.5
  294.1 0.6 copy.33
  294.7 0.0 copy-done.3
  294.7 0.7 copy.34
  295.4 0.0 copy-done.2
  295.4 0.7 copy.35
  (1 shorter events, 0.0 us)
Async XLA Ops:
  170.8 119.5 %copy-start = (bf16[4,256,768]{2,1,0:T(8,128)(2,1)S(1)}, bf16[4,256,768]{2,1,0:T(8,128)(2,1)}, u32[]{:S(2)}) copy-start(bf16[4,256,768]{2,1,0:T(8,128)(2,1)} %get-tuple-element.29) | copy-start | bytes 4718596
  290.2 2.0 copy-start.1
  292.2 1.2 copy-start.4
  292.2 1.9 copy-start.5
  292.2 2.5 copy-start.3
  292.2 3.2 %copy-start.2 = (f32[192,384]{1,0:T(8,128)S(1)}, f32[192,384]{1,0:T(8,128)}, u32[]{:S(2)}) copy-start(f32[192,384]{1,0:T(8,128)} %get-tuple-element.46) | copy-start | bytes 884740

commit v3 on v2

--- a/solution.py
+++ b/solution.py
@@ -727,7 +727,7 @@
     0: ("u20", "o00",), 1: ("u01", "u11",), 3: ("u21", "d13",), 4: ("d03",), 6: ("d23", "d14",), 7: ("d04",), 8: ("a0", "u02",), 9: ("o01", "d24", "d15",), 10: ("a1", "d05",),
     12: ("u12", "d25",), 14: ("u22", "u03",), 16: ("b0",), 17: ("u13", "u04",), 18: ("o02", "b1",), 20: ("u14", "u05",), 21: ("a2", "u23",), 22: ("u15",), 23: ("o03",),
 }
-PACE = ((0, 16), "c1", "a3", "b2", "u24", "o04", (16, 32), "c2", "a4", "b3", "c3", "b4", "c4")
+PACE = ((0, 16), "c0", "c1", "a3", "b2", "u24", "o04", (16, 32), "c2", "a4", "b3", "c3", "b4", "c4")
 LATE = ("o05", "u25")
 
 
@@ -1060,7 +1060,6 @@
         dxt_v[near] = total.astype(BF).reshape(half_groups, width // groups, rows)
 
     count = half_groups * n_col
-    table["c0"]()
     grad_input(0)
     made_parts = 1
     for step in PACE:

time: 296 us -> 294 us (level)
  Pallas kernels: 287 us -> 284 us
where the time goes in v3:
time: 294 us
  Pallas kernels  284 us (97%)
  local copies, waits for them, and re-layouts  7.81 us (3%)
    pallas_call x1, Pallas kernels, forward(): pl.pallas_call(functools.partial(forward_kernel, dims), out_shape=outs, i...  169 us
    pallas_call x1, Pallas kernels, backward(): pl.pallas_call(functools.partial(backward_kernel, dims, plan), out_shape=...  116 us
    unnamed x18, local copies, waits for them, and re-layouts  5.9 us

profile of v3, /device:TPU:0, one launch (start us, length us, event | category | flops | bytes accessed | tf_op | source)
XLA Modules:
  0.0 293.6 jit_solution(1180895430781476881)
XLA Ops:
  0.7 0.7 maximum_convert_fusion
  1.4 0.1 iota_compare_fusion
  1.5 0.1 select_reduce_fusion
  1.6 0.6 pad.4.norm_ref
  2.2 168.6 %forward_part.1 = (bf16[8,96,1024]{2,1,0:T(8,128)(2,1)}, bf16[8,2,48,2304]{3,2,1,0:T(8,128)(2,1)}, bf16[1024,2304]{1,0:T(8,128)(2,1)}, bf16[768,1024]{1,0:T(8,12...) custom-call(s32[4,8]{1,0:T(4,128)} %seq_ref.3, ...), custom_call_target="tpu_custom_call" | custom-call | tf_op jit(solution)/shard_map/forward_part/pallas_call | solution.py:690
  170.8 0.0 copy-start
  170.8 115.5 %backward_part.1 = (bf16[4,8,96,256]{3,2,1,0:T(8,128)(2,1)}, f32[96,576]{1,0:T(8,128)}, f32[96,192]{1,0:T(8,128)}, f32[96,768]{1,0:T(8,128)}, f32[192,384]{1,0:T(8,128)}, /*index=5*/f32[8,256]{1,0:T(8,128)}) custom-call(s32[4,8]{1,0:T(4,128)} %seq_ref.3, s32[4,8]{1,0:T(4,128)} %len_ref.3, bf16[1024,2304]{1,0:T(8,128)(2,1)} %get-tuple-element.30.qkv_ref, ...), custom_call_target="tpu_custom_call" | custom-call | tf_op jit(solution)/shard_map/backward_part/pallas_call | solution.py:1151
  286.3 0.8 constant_dynamic-slice_fusion
  287.1 0.5 slice_bitcast_fusion
  287.6 0.0 copy-done
  287.6 0.0 copy-start.1
  287.6 1.1 copy.30
  288.8 0.8 copy-done.1
  289.6 0.0 copy-start.4
  289.6 0.0 copy-start.5
  289.6 0.0 copy-start.3
  289.6 0.0 copy-start.2
  289.6 1.1 copy.31
  290.8 0.0 copy-done.4
  290.8 0.7 copy.32
  291.5 0.0 copy-done.5
  291.5 0.6 copy.33
  292.1 0.0 copy-done.3
  292.1 0.7 copy.34
  292.8 0.0 copy-done.2
  292.8 0.7 copy.35
  (1 shorter events, 0.0 us)
Async XLA Ops:
  170.8 116.9 %copy-start = (bf16[4,256,768]{2,1,0:T(8,128)(2,1)S(1)}, bf16[4,256,768]{2,1,0:T(8,128)(2,1)}, u32[]{:S(2)}) copy-start(bf16[4,256,768]{2,1,0:T(8,128)(2,1)} %get-tuple-element.29) | copy-start | bytes 4718596
  287.6 2.0 copy-start.1
  289.6 1.2 copy-start.4
  289.6 1.9 copy-start.5
  289.6 2.5 copy-start.3
  289.6 3.2 %copy-start.2 = (f32[192,384]{1,0:T(8,128)S(1)}, f32[192,384]{1,0:T(8,128)}, u32[]{:S(2)}) copy-start(f32[192,384]{1,0:T(8,128)} %get-tuple-element.46) | copy-start | bytes 884740

commit v4 on v3

--- a/solution.py
+++ b/solution.py
@@ -249,7 +249,7 @@
     "project": {0: ("of", "v3", "d2",), 3: ("uf", "d3",), 6: ("vf", "ez",)},
     "attend": {0: ("df", "os", "e1",), 1: ("e2",), 2: ("us", "e3",), 3: ("ot", "ut",), 4: ("ef",), 5: ("vs",), 6: ("vt",), 7: ("c1",), 8: ("c2", "c3",), 9: ("ds",), 11: ("dt",)},
     "mix": {1: ("es",)},
-    "rise": {0: ("et",)},
+    "rise": {3: ("et",)},
 }
 
 

time: 294 us -> 294 us (level)
  no operation moved by 1% of the time
where the time goes in v4:
time: 294 us
  Pallas kernels  284 us (97%)
  local copies, waits for them, and re-layouts  7.81 us (3%)
    pallas_call x1, Pallas kernels, forward(): pl.pallas_call(functools.partial(forward_kernel, dims), out_shape=outs, i...  169 us
    pallas_call x1, Pallas kernels, backward(): pl.pallas_call(functools.partial(backward_kernel, dims, plan), out_shape=...  115 us
    unnamed x18, local copies, waits for them, and re-layouts  5.9 us

profile of v4, /device:TPU:0, one launch (start us, length us, event | category | flops | bytes accessed | tf_op | source)
XLA Modules:
  0.0 293.5 jit_solution(2907286631491049649)
XLA Ops:
  0.7 0.7 maximum_convert_fusion
  1.4 0.1 iota_compare_fusion
  1.5 0.1 select_reduce_fusion
  1.6 0.6 pad.4.norm_ref
  2.2 168.6 %forward_part.1 = (bf16[8,96,1024]{2,1,0:T(8,128)(2,1)}, bf16[8,2,48,2304]{3,2,1,0:T(8,128)(2,1)}, bf16[1024,2304]{1,0:T(8,128)(2,1)}, bf16[768,1024]{1,0:T(8,12...) custom-call(s32[4,8]{1,0:T(4,128)} %seq_ref.3, ...), custom_call_target="tpu_custom_call" | custom-call | tf_op jit(solution)/shard_map/forward_part/pallas_call | solution.py:690
  170.8 0.0 copy-start
  170.8 115.5 %backward_part.1 = (bf16[4,8,96,256]{3,2,1,0:T(8,128)(2,1)}, f32[96,576]{1,0:T(8,128)}, f32[96,192]{1,0:T(8,128)}, f32[96,768]{1,0:T(8,128)}, f32[192,384]{1,0:T(8,128)}, /*index=5*/f32[8,256]{1,0:T(8,128)}) custom-call(s32[4,8]{1,0:T(4,128)} %seq_ref.3, s32[4,8]{1,0:T(4,128)} %len_ref.3, bf16[1024,2304]{1,0:T(8,128)(2,1)} %get-tuple-element.30.qkv_ref, ...), custom_call_target="tpu_custom_call" | custom-call | tf_op jit(solution)/shard_map/backward_part/pallas_call | solution.py:1151
  286.3 0.8 constant_dynamic-slice_fusion
  287.1 0.5 slice_bitcast_fusion
  287.6 0.0 copy-done
  287.6 0.0 copy-start.1
  287.6 1.1 copy.30
  288.7 0.8 copy-done.1
  289.6 0.0 copy-start.4
  289.6 0.0 copy-start.5
  289.6 0.0 copy-start.3
  289.6 0.0 copy-start.2
  289.6 1.1 copy.31
  290.7 0.0 copy-done.4
  290.7 0.7 copy.32
  291.4 0.0 copy-done.5
  291.4 0.6 copy.33
  292.1 0.0 copy-done.3
  292.1 0.7 copy.34
  292.8 0.0 copy-done.2
  292.8 0.7 copy.35
  (1 shorter events, 0.0 us)
Async XLA Ops:
  170.8 116.8 %copy-start = (bf16[4,256,768]{2,1,0:T(8,128)(2,1)S(1)}, bf16[4,256,768]{2,1,0:T(8,128)(2,1)}, u32[]{:S(2)}) copy-start(bf16[4,256,768]{2,1,0:T(8,128)(2,1)} %get-tuple-element.29) | copy-start | bytes 4718596
  287.6 2.0 copy-start.1
  289.6 1.2 copy-start.4
  289.6 1.9 copy-start.5
  289.6 2.5 copy-start.3
  289.6 3.2 %copy-start.2 = (f32[192,384]{1,0:T(8,128)S(1)}, f32[192,384]{1,0:T(8,128)}, u32[]{:S(2)}) copy-start(f32[192,384]{1,0:T(8,128)} %get-tuple-element.46) | copy-start | bytes 884740
